TPU v7x, 32 devices: a whole 2x2x4 slice. The times are simulated.
32 devices in a mesh: groups: 2 (over x), slab: 16 (over z, y, core).
Axes of the slice: x: 2, y: 2, z: 4, core: 2. Of those that a mesh axis runs over, the one named last changes fastest.
Arguments:
- melt_speeds: float32 [3, 64, 32, 512], P(None, ('groups', 'slab')), parts along dimension 1, may hold values from -3 to 3
- heat_state: float32 [64, 32, 512], P(('groups', 'slab')), parts along dimension 0, may hold values from -4 to 4
- eddy_quantities: float32 [2, 64, 32, 512], P(None, ('groups', 'slab')), parts along dimension 1, may hold values from 0.02 to 1
- zone_labels: int32 [32, 16, 256], P(('groups', 'slab')), parts along dimension 0, may hold values from 0 to 7
- zone_resistivity_inverse: float32 [8], replicated, may hold values from 0.05 to 0.4
- imposed_induction: float32 [3, 512, 16, 16], P(None, ('groups', 'slab')), parts along dimension 1, may hold values from -4 to 4
- winding_current: float32 [3, 512, 16, 16], P(None, ('groups', 'slab')), parts along dimension 1, may hold values from -4 to 4
- window_entry_induction_guess: float32 [3, 512, 16, 16], P(None, ('groups', 'slab')), parts along dimension 1, may hold values from 1 to 4
Outputs:
- velocity_out: float32 [3, 64, 32, 512], P(None, ('groups', 'slab')), parts along dimension 1
- temperature_out: float32 [64, 32, 512], P(('groups', 'slab')), parts along dimension 0
- turbulence_out: float32 [2, 64, 32, 512], P(None, ('groups', 'slab')), parts along dimension 1
- potential: float32 [3, 512, 16, 16], P(None, ('groups', 'slab')), parts along dimension 1
There are 2 independent parts, one for each index of `groups`. A program takes and returns all parts, laid end to end along the dimension named above; an argument that names none is the same for every part. Nothing has to cross between parts.
Inputs may be any that keep to these rules, and one draw needn't show every extreme that they name: `zone_labels`: region number of each coarse block.
All inputs are finite; a program needn't handle non-finite values.
Results may differ from a plain program's by a relative error of at most 0.0001.
Values sent between devices are 32-bit elements; how exact they have to be, the bound alone decides.
A program may use at most 128 MiB of HBM per device.

v0:
```python
import jax
import jax.numpy as jnp
from jax import lax
from jax.sharding import PartitionSpec as P

STEPS = 2
SWEEPS = 8


time_step = 0.02
molecular = 0.01
heat_diffuse = 0.01
eddy_coeff = 0.09
prod_coeff = 1.44
dissip_coeff = 1.92
turb_floor = 0.05
coupling = 1.0
thermal_gradient_factor = 0.3


def extended(block, sides, width):
    for axis, dim in sides:
        count = lax.axis_size(axis)
        forward = [(i, i + 1) for i in range(count - 1)]
        backward = [(target, source) for source, target in forward]
        low = lax.ppermute(
            lax.slice_in_dim(block, block.shape[dim] - width, None, axis=dim), axis, forward
        )
        high = lax.ppermute(lax.slice_in_dim(block, 0, width, axis=dim), axis, backward)
        block = jnp.concatenate([low, block, high], axis=dim)
    return block


def reduce_onto_parent(block):
    comps, depth, rows, cols = block.shape
    shaped = block.reshape(comps, depth // 2, 2, rows // 2, 2, cols // 2, 2)
    return jnp.mean(shaped, axis=(2, 4, 6))


def prolong(block):
    comps, depth, rows, cols = block.shape
    wide = jnp.broadcast_to(
        block[:, :, None, :, None, :, None], (comps, depth, 2, rows, 2, cols, 2)
    )
    return wide.reshape(comps, depth * 2, rows * 2, cols * 2)


def cross(left_vec, right_vec):
    return jnp.stack(
        [
            left_vec[1] * right_vec[2] - left_vec[2] * right_vec[1],
            left_vec[2] * right_vec[0] - left_vec[0] * right_vec[2],
            left_vec[0] * right_vec[1] - left_vec[1] * right_vec[0],
        ],
        0,
    )


def neighbours(padded):
    return (
        padded[:, 2:, 1:-1, 1:-1]
        + padded[:, :-2, 1:-1, 1:-1]
        + padded[:, 1:-1, 2:, 1:-1]
        + padded[:, 1:-1, :-2, 1:-1]
        + padded[:, 1:-1, 1:-1, 2:]
        + padded[:, 1:-1, 1:-1, :-2]
    )


def ohmic_admittance(zone_labels, zone_resistivity_inverse, heat_state):
    labels = jnp.arange(zone_resistivity_inverse.shape[0], dtype=jnp.int32)
    onehot = zone_labels[None] == labels[:, None, None, None]
    searched_higher = jnp.sum(
        jnp.where(onehot, zone_resistivity_inverse[:, None, None, None], jnp.float32(0.0)), axis=0
    )
    return (
        searched_higher
        * reduce_onto_parent(jnp.exp(-thermal_gradient_factor * heat_state)[None])[0]
    )


def faces(potential):
    padded = extended(potential, (("slab", 1),), 1)
    return jnp.pad(padded, ((0, 0), (0, 0), (1, 1), (1, 1)))


def relax(coupled, imposed_induction, winding_current, potential):
    conduct = coupled[3]
    motional = cross(coupled[:3], imposed_induction)
    source = conduct * motional + winding_current
    diagonal = 6.0 + coupling * conduct
    for sweep_index in range(SWEEPS):
        potential = (source + neighbours(faces(potential))) / diagonal
    drive_field = motional - coupling * potential
    current = conduct * drive_field + winding_current
    lorentz = cross(current, imposed_induction)
    joule = conduct * jnp.sum(drive_field * drive_field, axis=0)
    return (potential, jnp.concatenate([lorentz, joule[None]], 0))


def advance(padded, lorentz, joule):
    bordered = jnp.pad(padded, ((0, 0), (0, 0), (0, 0), (1, 1)))
    center = bordered[:, 1:-1, 1:-1, 1:-1]
    z_plus = bordered[:, 2:, 1:-1, 1:-1]
    z_minus = bordered[:, :-2, 1:-1, 1:-1]
    y_plus = bordered[:, 1:-1, 2:, 1:-1]
    y_minus = bordered[:, 1:-1, :-2, 1:-1]
    x_plus = bordered[:, 1:-1, 1:-1, 2:]
    x_minus = bordered[:, 1:-1, 1:-1, :-2]
    grad_z = 0.5 * (z_plus - z_minus)
    grad_y = 0.5 * (y_plus - y_minus)
    grad_x = 0.5 * (x_plus - x_minus)
    laplace = z_plus + z_minus + y_plus + y_minus + x_plus + x_minus - 6.0 * center
    kinetic = center[4]
    dissip = center[5]
    transport = center[0] * grad_x + center[1] * grad_y + center[2] * grad_z
    eddy_visc = eddy_coeff * kinetic * kinetic / jnp.maximum(dissip, turb_floor)
    strain = jnp.sum(
        grad_x[:3] * grad_x[:3] + grad_y[:3] * grad_y[:3] + grad_z[:3] * grad_z[:3], axis=0
    )
    produce = eddy_visc * strain
    diffuse = jnp.stack(
        [
            molecular + eddy_visc,
            molecular + eddy_visc,
            molecular + eddy_visc,
            heat_diffuse + eddy_visc / 0.9,
            molecular + eddy_visc,
            molecular + eddy_visc / 1.3,
        ],
        0,
    )
    dissip_source = (
        (prod_coeff * produce - dissip_coeff * dissip) * dissip / jnp.maximum(kinetic, turb_floor)
    )
    source = jnp.concatenate(
        [lorentz, joule[None], (produce - dissip)[None], dissip_source[None]], 0
    )
    return center + time_step * (diffuse * laplace - transport + source)


def flow_step(induction_tables, em_loads):
    padded = extended(induction_tables, (("slab", 1),), 1)
    padded = jnp.pad(padded, ((0, 0), (0, 0), (1, 1), (0, 0)))
    return advance(padded, em_loads[:3], em_loads[3])


def local_coupled(induction_tables, zone_labels, zone_resistivity_inverse):
    conduct = ohmic_admittance(zone_labels, zone_resistivity_inverse, induction_tables[3])
    return jnp.concatenate([reduce_onto_parent(induction_tables[:3]), conduct[None]], 0)


def on_device(
    melt_speeds,
    heat_state,
    eddy_quantities,
    zone_labels,
    zone_resistivity_inverse,
    imposed_induction,
    winding_current,
    window_entry_induction_guess,
):
    induction_tables = jnp.concatenate([melt_speeds, heat_state[None], eddy_quantities], 0)
    arrived = (
        lax.all_to_all(
            window_entry_induction_guess, "slab", split_axis=3, concat_axis=1, tiled=True
        ),
        lax.all_to_all(imposed_induction, "slab", split_axis=3, concat_axis=1, tiled=True),
        lax.all_to_all(winding_current, "slab", split_axis=3, concat_axis=1, tiled=True),
    )
    potential = jnp.transpose(arrived[0], (0, 3, 2, 1))
    field_local = jnp.transpose(arrived[1], (0, 3, 2, 1))
    coil_local = jnp.transpose(arrived[2], (0, 3, 2, 1))
    for step_index in range(STEPS):
        coupled = local_coupled(induction_tables, zone_labels, zone_resistivity_inverse)
        potential, em_loads = relax(coupled, field_local, coil_local, potential)
        induction_tables = flow_step(induction_tables, prolong(em_loads))
    potential = lax.all_to_all(
        jnp.transpose(potential, (0, 3, 2, 1)), "slab", split_axis=1, concat_axis=3, tiled=True
    )
    return (induction_tables[:3], induction_tables[3], induction_tables[4:], potential)


def solution(mesh):
    return jax.shard_map(
        on_device,
        mesh=mesh,
        in_specs=(
            P(None, ("groups", "slab"), None, None),
            P(("groups", "slab"), None, None),
            P(None, ("groups", "slab"), None, None),
            P(("groups", "slab"), None, None),
            P(),
            P(None, ("groups", "slab"), None, None),
            P(None, ("groups", "slab"), None, None),
            P(None, ("groups", "slab"), None, None),
        ),
        out_specs=(
            P(None, ("groups", "slab"), None, None),
            P(("groups", "slab"), None, None),
            P(None, ("groups", "slab"), None, None),
            P(None, ("groups", "slab"), None, None),
        ),
        check_vma=False,
    )
```

profile of v0, /device:TPU:0, one launch (start us, length us, event | category | flops | bytes accessed | tf_op | source)
XLA Modules:
  0.0 315.9 jit_solution(1965931268456075200)
XLA Ops:
  2.7 7.4 %all-to-all-start.2 = ((f32[16,1,768]{2,1,0:T(1,128)}), f32[16,1,768]{2,1,0:T(1,128)}, u32[]{:S(2)}, u32[]{:S(2)}) async-start(f32[16,1,768]{2,1,0:T(1,128)} %reshape.394), calls=%async_computation.2 | async-start | bytes 98304 | tf_op jit(solution)/shard_map/all_to_all | solution.py:165
  16.6 14.0 %reduce_sum.122 = f32[3,16,2,256,2]{4,3,2,1,0:T(8,128)} reshape(f32[3,32,512]{2,1,0:T(8,128)S(1)} %reduce_sum.121) | data formatting | bytes 393216 | tf_op jit(solution)/shard_map/reduce_sum | solution.py:37
  30.6 6.3 %reduce_sum.123 = f32[3,16,256]{2,1,0:T(8,128)S(1)} reduce(f32[3,16,2,256,2]{4,3,2,1,0:T(8,128)} %reduce_sum.122, f32[]{:T(128)} %constant.11.clone.1), dimensions={2,4}, to_apply=%region_4.5 | reduce | flops 36864 | bytes 245764 | tf_op jit(solution)/shard_map/reduce_sum | solution.py:37
  37.5 5.5 %reduce_sum.119 = f32[16,2,256,2]{3,2,1,0:T(8,128)} reshape(f32[32,512]{1,0:T(8,128)S(1)} %exponential_reduce_fusion) | data formatting | bytes 131072 | tf_op jit(solution)/shard_map/reduce_sum | solution.py:37
  48.7 6.9 %all-to-all-start = ((f32[16,1,768]{2,1,0:T(1,128)}), f32[16,1,768]{2,1,0:T(1,128)S(1)}, u32[]{:S(2)}, u32[]{:S(2)}) async-start(f32[16,1,768]{2,1,0:T(1,128)} %reshape.392), calls=%async_computation | async-start | bytes 98304 | tf_op jit(solution)/shard_map/all_to_all | solution.py:168
  62.8 7.1 %all-to-all-start.1 = ((f32[16,1,768]{2,1,0:T(1,128)}), f32[16,1,768]{2,1,0:T(1,128)}, u32[]{:S(2)}, u32[]{:S(2)}) async-start(f32[16,1,768]{2,1,0:T(1,128)} %reshape.390), calls=%async_computation.1 | async-start | bytes 98304 | tf_op jit(solution)/shard_map/all_to_all | solution.py:169
  71.2 5.4 %all-to-all-done.1 = f32[16,1,768]{2,1,0:T(1,128)} async-done(((f32[16,1,768]{2,1,0:T(1,128)}), f32[16,1,768]{2,1,0:T(1,128)}, u32[]{:S(2)}, u32[]{:S(2)}) %all-to-all-start.1) | async-done | bytes 49184 | tf_op jit(solution)/shard_map/all_to_all | solution.py:169
  99.7 5.6 %collective-permute-start.11 = (f32[3,1,16,256]{3,2,1,0:T(8,128)S(1)}, f32[3,1,16,256]{3,2,1,0:T(8,128)S(1)}, u32[]{:S(2)}, u32[]{:S(2)}) collective-permute-start(f32[3,1,16,256]{3,2,1,0:T(8,128)S(1)} %fusion.57), channel_id=1, source_target_pairs={{0,1},{1,2},{2,3},{3,4},{4,5},{5,6},{6,7},{7,8},{8,9},{9,10},{10,1... | collective-permute-start | bytes 147464 | tf_op jit(solution)/shard_map/ppermute | solution.py:26
  107.7 5.3 %collective-permute-start.13 = (f32[3,1,16,256]{3,2,1,0:T(8,128)S(1)}, f32[3,1,16,256]{3,2,1,0:T(8,128)S(1)}, u32[]{:S(2)}, u32[]{:S(2)}) collective-permute-start(f32[3,1,16,256]{3,2,1,0:T(8,128)S(1)} %fusion.55), channel_id=1, source_target_pairs={{0,1},{1,2},{2,3},{3,4},{4,5},{5,6},{6,7},{7,8},{8,9},{9,10},{10,1... | collective-permute-start | bytes 147464 | tf_op jit(solution)/shard_map/ppermute | solution.py:26
  115.5 5.4 %collective-permute-start.15 = (f32[3,1,16,256]{3,2,1,0:T(8,128)S(1)}, f32[3,1,16,256]{3,2,1,0:T(8,128)S(1)}, u32[]{:S(2)}, u32[]{:S(2)}) collective-permute-start(f32[3,1,16,256]{3,2,1,0:T(8,128)S(1)} %fusion.53), channel_id=1, source_target_pairs={{0,1},{1,2},{2,3},{3,4},{4,5},{5,6},{6,7},{7,8},{8,9},{9,10},{10,1... | collective-permute-start | bytes 147464 | tf_op jit(solution)/shard_map/ppermute | solution.py:26
  134.4 5.9 %collective-permute-start.21 = (f32[3,1,16,256]{3,2,1,0:T(8,128)}, f32[3,1,16,256]{3,2,1,0:T(8,128)}, u32[]{:S(2)}, u32[]{:S(2)}) collective-permute-start(f32[3,1,16,256]{3,2,1,0:T(8,128)} %get-tuple-element.31), channel_id=1, source_target_pairs={{0,1},{1,2},{2,3},{3,4},{4,5},{5,6},{6,7},{7,8},{8,9},{9,10},{10,1... | collective-permute-start | bytes 147464 | tf_op jit(solution)/shard_map/ppermute | solution.py:26
  146.5 9.8 %broadcast_in_dim.46 = f32[3,32,512]{2,1,0:T(8,128)S(1)} reshape(f32[3,16,2,256,2]{4,3,2,1,0:T(8,128)} %broadcast_in_dim.45) | data formatting | bytes 393216 | tf_op jit(solution)/shard_map/broadcast_in_dim | solution.py:42
  167.0 14.0 %reduce_sum.131 = f32[3,16,2,256,2]{4,3,2,1,0:T(8,128)} reshape(f32[3,32,512]{2,1,0:T(8,128)S(1)} %slice_reduce_fusion) | data formatting | bytes 393216 | tf_op jit(solution)/shard_map/reduce_sum | solution.py:37
  180.9 6.3 %reduce_sum.132 = f32[3,16,256]{2,1,0:T(8,128)S(1)} reduce(f32[3,16,2,256,2]{4,3,2,1,0:T(8,128)} %reduce_sum.131, f32[]{:T(128)} %constant.11.clone.1), dimensions={2,4}, to_apply=%region_10.11 | reduce | flops 36864 | bytes 245764 | tf_op jit(solution)/shard_map/reduce_sum | solution.py:37
  187.3 5.5 %reduce_sum.128 = f32[16,2,256,2]{3,2,1,0:T(8,128)} reshape(f32[32,512]{1,0:T(8,128)S(1)} %get-tuple-element.45) | data formatting | bytes 131072 | tf_op jit(solution)/shard_map/reduce_sum | solution.py:37
  206.5 5.8 %collective-permute-start.25 = (f32[3,1,16,256]{3,2,1,0:T(8,128)S(1)}, f32[3,1,16,256]{3,2,1,0:T(8,128)S(1)}, u32[]{:S(2)}, u32[]{:S(2)}) collective-permute-start(f32[3,1,16,256]{3,2,1,0:T(8,128)S(1)} %fusion.45), channel_id=1, source_target_pairs={{0,1},{1,2},{2,3},{3,4},{4,5},{5,6},{6,7},{7,8},{8,9},{9,10},{10,1... | collective-permute-start | bytes 147464 | tf_op jit(solution)/shard_map/ppermute | solution.py:26
  214.7 5.8 %collective-permute-start.27 = (f32[3,1,16,256]{3,2,1,0:T(8,128)S(1)}, f32[3,1,16,256]{3,2,1,0:T(8,128)S(1)}, u32[]{:S(2)}, u32[]{:S(2)}) collective-permute-start(f32[3,1,16,256]{3,2,1,0:T(8,128)S(1)} %fusion.43), channel_id=1, source_target_pairs={{0,1},{1,2},{2,3},{3,4},{4,5},{5,6},{6,7},{7,8},{8,9},{9,10},{10,1... | collective-permute-start | bytes 147464 | tf_op jit(solution)/shard_map/ppermute | solution.py:26
  222.9 5.5 %collective-permute-start.29 = (f32[3,1,16,256]{3,2,1,0:T(8,128)S(1)}, f32[3,1,16,256]{3,2,1,0:T(8,128)S(1)}, u32[]{:S(2)}, u32[]{:S(2)}) collective-permute-start(f32[3,1,16,256]{3,2,1,0:T(8,128)S(1)} %fusion.41), channel_id=1, source_target_pairs={{0,1},{1,2},{2,3},{3,4},{4,5},{5,6},{6,7},{7,8},{8,9},{9,10},{10,1... | collective-permute-start | bytes 147464 | tf_op jit(solution)/shard_map/ppermute | solution.py:26
  230.9 6.1 %collective-permute-start.31 = (f32[3,1,16,256]{3,2,1,0:T(8,128)S(1)}, f32[3,1,16,256]{3,2,1,0:T(8,128)S(1)}, u32[]{:S(2)}, u32[]{:S(2)}) collective-permute-start(f32[3,1,16,256]{3,2,1,0:T(8,128)S(1)} %fusion.39), channel_id=1, source_target_pairs={{0,1},{1,2},{2,3},{3,4},{4,5},{5,6},{6,7},{7,8},{8,9},{9,10},{10,1... | collective-permute-start | bytes 147464 | tf_op jit(solution)/shard_map/ppermute | solution.py:26
  238.3 5.8 %collective-permute-start.19 = (f32[6,1,32,512]{3,2,1,0:T(8,128)S(1)}, f32[6,1,32,512]{3,2,1,0:T(8,128)S(1)}, u32[]{:S(2)}, u32[]{:S(2)}) collective-permute-start(f32[6,1,32,512]{3,2,1,0:T(8,128)S(1)} %get-tuple-element.46), channel_id=1, source_target_pairs={{0,1},{1,2},{2,3},{3,4},{4,5},{5,6},{6,7},{7,8},{8,9},{9,10},{10,1... | collective-permute-start | bytes 1179656 | tf_op jit(solution)/shard_map/ppermute | solution.py:26
  245.7 6.0 %collective-permute-start.33 = (f32[3,1,16,256]{3,2,1,0:T(8,128)S(1)}, f32[3,1,16,256]{3,2,1,0:T(8,128)S(1)}, u32[]{:S(2)}, u32[]{:S(2)}) collective-permute-start(f32[3,1,16,256]{3,2,1,0:T(8,128)S(1)} %fusion.37), channel_id=1, source_target_pairs={{0,1},{1,2},{2,3},{3,4},{4,5},{5,6},{6,7},{7,8},{8,9},{9,10},{10,1... | collective-permute-start | bytes 147464 | tf_op jit(solution)/shard_map/ppermute | solution.py:26
  254.2 7.0 %collective-permute-start.35 = (f32[3,1,16,256]{3,2,1,0:T(8,128)S(1)}, f32[3,1,16,256]{3,2,1,0:T(8,128)S(1)}, u32[]{:S(2)}, u32[]{:S(2)}) collective-permute-start(f32[3,1,16,256]{3,2,1,0:T(8,128)S(1)} %fusion.35), channel_id=1, source_target_pairs={{0,1},{1,2},{2,3},{3,4},{4,5},{5,6},{6,7},{7,8},{8,9},{9,10},{10,1... | collective-permute-start | bytes 147464 | tf_op jit(solution)/shard_map/ppermute | solution.py:26
  270.3 10.3 %broadcast_in_dim.91 = f32[3,32,512]{2,1,0:T(8,128)} reshape(f32[3,16,2,256,2]{4,3,2,1,0:T(8,128)} %broadcast_in_dim.90) | data formatting | bytes 393216 | tf_op jit(solution)/shard_map/broadcast_in_dim | solution.py:42
  296.5 8.9 %all-to-all-start.3 = ((f32[16,1,768]{2,1,0:T(1,128)}), f32[16,1,768]{2,1,0:T(1,128)}, u32[]{:S(2)}, u32[]{:S(2)}) async-start(f32[16,1,768]{2,1,0:T(1,128)} %reshape.396), calls=%async_computation.3 | async-start | bytes 98304 | tf_op jit(solution)/shard_map/all_to_all | solution.py:178
  (270 shorter events, 142.1 us)
Async XLA Ops:
  2.7 46.0 %all-to-all-start.2 = ((f32[16,1,768]{2,1,0:T(1,128)}), f32[16,1,768]{2,1,0:T(1,128)}, u32[]{:S(2)}, u32[]{:S(2)}) async-start(f32[16,1,768]{2,1,0:T(1,128)} %reshape.394), calls=%async_computation.2 | async-start | bytes 98304 | tf_op jit(solution)/shard_map/all_to_all | solution.py:165
  11.4 109.5 %collective-permute-start = (f32[6,1,32,512]{3,2,1,0:T(8,128)S(1)}, f32[6,1,32,512]{3,2,1,0:T(8,128)S(1)}, u32[]{:S(2)}, u32[]{:S(2)}) collective-permute-start(f32[6,1,32,512]{3,2,1,0:T(8,128)S(1)} %get-tuple-element.49), channel_id=1, source_target_pairs={{1,0},{2,1},{3,2},{4,3},{5,4},{6,5},{7,6},{8,7},{9,8},{10,9},{11,1... | collective-permute-start | bytes 1179656 | tf_op jit(solution)/shard_map/ppermute | solution.py:29
  12.7 108.2 %collective-permute-start.1 = (f32[6,1,32,512]{3,2,1,0:T(8,128)S(1)}, f32[6,1,32,512]{3,2,1,0:T(8,128)S(1)}, u32[]{:S(2)}, u32[]{:S(2)}) collective-permute-start(f32[6,1,32,512]{3,2,1,0:T(8,128)S(1)} %get-tuple-element.48), channel_id=1, source_target_pairs={{0,1},{1,2},{2,3},{3,4},{4,5},{5,6},{6,7},{7,8},{8,9},{9,10},{10,1... | collective-permute-start | bytes 1179656 | tf_op jit(solution)/shard_map/ppermute | solution.py:26
  48.7 14.0 %all-to-all-start = ((f32[16,1,768]{2,1,0:T(1,128)}), f32[16,1,768]{2,1,0:T(1,128)S(1)}, u32[]{:S(2)}, u32[]{:S(2)}) async-start(f32[16,1,768]{2,1,0:T(1,128)} %reshape.392), calls=%async_computation | async-start | bytes 98304 | tf_op jit(solution)/shard_map/all_to_all | solution.py:168
  58.4 20.5 %collective-permute-start.2 = (f32[3,1,16,256]{3,2,1,0:T(8,128)S(1)}, f32[3,1,16,256]{3,2,1,0:T(8,128)S(1)}, u32[]{:S(2)}, u32[]{:S(2)}) collective-permute-start(f32[3,1,16,256]{3,2,1,0:T(8,128)S(1)} %bitcast.204), channel_id=1, source_target_pairs={{1,0},{2,1},{3,2},{4,3},{5,4},{6,5},{7,6},{8,7},{9,8},{10,9},{11,1... | collective-permute-start | bytes 147464 | tf_op jit(solution)/shard_map/ppermute | solution.py:29
  59.7 19.2 %collective-permute-start.3 = (f32[3,1,16,256]{3,2,1,0:T(8,128)S(1)}, f32[3,1,16,256]{3,2,1,0:T(8,128)S(1)}, u32[]{:S(2)}, u32[]{:S(2)}) collective-permute-start(f32[3,1,16,256]{3,2,1,0:T(8,128)S(1)} %bitcast.205), channel_id=1, source_target_pairs={{0,1},{1,2},{2,3},{3,4},{4,5},{5,6},{6,7},{7,8},{8,9},{9,10},{10,1... | collective-permute-start | bytes 147464 | tf_op jit(solution)/shard_map/ppermute | solution.py:26
  62.8 13.9 %all-to-all-start.1 = ((f32[16,1,768]{2,1,0:T(1,128)}), f32[16,1,768]{2,1,0:T(1,128)}, u32[]{:S(2)}, u32[]{:S(2)}) async-start(f32[16,1,768]{2,1,0:T(1,128)} %reshape.390), calls=%async_computation.1 | async-start | bytes 98304 | tf_op jit(solution)/shard_map/all_to_all | solution.py:169
  98.4 6.9 %collective-permute-start.10 = (f32[3,1,16,256]{3,2,1,0:T(8,128)S(1)}, f32[3,1,16,256]{3,2,1,0:T(8,128)S(1)}, u32[]{:S(2)}, u32[]{:S(2)}) collective-permute-start(f32[3,1,16,256]{3,2,1,0:T(8,128)S(1)} %fusion.57), channel_id=1, source_target_pairs={{1,0},{2,1},{3,2},{4,3},{5,4},{6,5},{7,6},{8,7},{9,8},{10,9},{11,1... | collective-permute-start | bytes 147464 | tf_op jit(solution)/shard_map/ppermute | solution.py:29
  114.2 10.7 %collective-permute-start.14 = (f32[3,1,16,256]{3,2,1,0:T(8,128)S(1)}, f32[3,1,16,256]{3,2,1,0:T(8,128)S(1)}, u32[]{:S(2)}, u32[]{:S(2)}) collective-permute-start(f32[3,1,16,256]{3,2,1,0:T(8,128)S(1)} %fusion.53), channel_id=1, source_target_pairs={{1,0},{2,1},{3,2},{4,3},{5,4},{6,5},{7,6},{8,7},{9,8},{10,9},{11,1... | collective-permute-start | bytes 147464 | tf_op jit(solution)/shard_map/ppermute | solution.py:29
  115.5 9.4 %collective-permute-start.15 = (f32[3,1,16,256]{3,2,1,0:T(8,128)S(1)}, f32[3,1,16,256]{3,2,1,0:T(8,128)S(1)}, u32[]{:S(2)}, u32[]{:S(2)}) collective-permute-start(f32[3,1,16,256]{3,2,1,0:T(8,128)S(1)} %fusion.53), channel_id=1, source_target_pairs={{0,1},{1,2},{2,3},{3,4},{4,5},{5,6},{6,7},{7,8},{8,9},{9,10},{10,1... | collective-permute-start | bytes 147464 | tf_op jit(solution)/shard_map/ppermute | solution.py:26
  125.2 6.9 %collective-permute-start.16 = (f32[3,1,16,256]{3,2,1,0:T(8,128)S(1)}, f32[3,1,16,256]{3,2,1,0:T(8,128)S(1)}, u32[]{:S(2)}, u32[]{:S(2)}) collective-permute-start(f32[3,1,16,256]{3,2,1,0:T(8,128)S(1)} %fusion.51), channel_id=1, source_target_pairs={{1,0},{2,1},{3,2},{4,3},{5,4},{6,5},{7,6},{8,7},{9,8},{10,9},{11,1... | collective-permute-start | bytes 147464 | tf_op jit(solution)/shard_map/ppermute | solution.py:29
  133.2 62.5 %collective-permute-start.20 = (f32[3,1,16,256]{3,2,1,0:T(8,128)}, f32[3,1,16,256]{3,2,1,0:T(8,128)}, u32[]{:S(2)}, u32[]{:S(2)}) collective-permute-start(f32[3,1,16,256]{3,2,1,0:T(8,128)} %get-tuple-element.31), channel_id=1, source_target_pairs={{1,0},{2,1},{3,2},{4,3},{5,4},{6,5},{7,6},{8,7},{9,8},{10,9},{11,1... | collective-permute-start | bytes 147464 | tf_op jit(solution)/shard_map/ppermute | solution.py:29
  134.4 61.3 %collective-permute-start.21 = (f32[3,1,16,256]{3,2,1,0:T(8,128)}, f32[3,1,16,256]{3,2,1,0:T(8,128)}, u32[]{:S(2)}, u32[]{:S(2)}) collective-permute-start(f32[3,1,16,256]{3,2,1,0:T(8,128)} %get-tuple-element.31), channel_id=1, source_target_pairs={{0,1},{1,2},{2,3},{3,4},{4,5},{5,6},{6,7},{7,8},{8,9},{9,10},{10,1... | collective-permute-start | bytes 147464 | tf_op jit(solution)/shard_map/ppermute | solution.py:26
  205.2 7.1 %collective-permute-start.24 = (f32[3,1,16,256]{3,2,1,0:T(8,128)S(1)}, f32[3,1,16,256]{3,2,1,0:T(8,128)S(1)}, u32[]{:S(2)}, u32[]{:S(2)}) collective-permute-start(f32[3,1,16,256]{3,2,1,0:T(8,128)S(1)} %fusion.45), channel_id=1, source_target_pairs={{1,0},{2,1},{3,2},{4,3},{5,4},{6,5},{7,6},{8,7},{9,8},{10,9},{11,1... | collective-permute-start | bytes 147464 | tf_op jit(solution)/shard_map/ppermute | solution.py:29
  213.4 7.1 %collective-permute-start.26 = (f32[3,1,16,256]{3,2,1,0:T(8,128)S(1)}, f32[3,1,16,256]{3,2,1,0:T(8,128)S(1)}, u32[]{:S(2)}, u32[]{:S(2)}) collective-permute-start(f32[3,1,16,256]{3,2,1,0:T(8,128)S(1)} %fusion.43), channel_id=1, source_target_pairs={{1,0},{2,1},{3,2},{4,3},{5,4},{6,5},{7,6},{8,7},{9,8},{10,9},{11,1... | collective-permute-start | bytes 147464 | tf_op jit(solution)/shard_map/ppermute | solution.py:29
  229.6 14.5 %collective-permute-start.30 = (f32[3,1,16,256]{3,2,1,0:T(8,128)S(1)}, f32[3,1,16,256]{3,2,1,0:T(8,128)S(1)}, u32[]{:S(2)}, u32[]{:S(2)}) collective-permute-start(f32[3,1,16,256]{3,2,1,0:T(8,128)S(1)} %fusion.39), channel_id=1, source_target_pairs={{1,0},{2,1},{3,2},{4,3},{5,4},{6,5},{7,6},{8,7},{9,8},{10,9},{11,1... | collective-permute-start | bytes 147464 | tf_op jit(solution)/shard_map/ppermute | solution.py:29
  230.9 13.2 %collective-permute-start.31 = (f32[3,1,16,256]{3,2,1,0:T(8,128)S(1)}, f32[3,1,16,256]{3,2,1,0:T(8,128)S(1)}, u32[]{:S(2)}, u32[]{:S(2)}) collective-permute-start(f32[3,1,16,256]{3,2,1,0:T(8,128)S(1)} %fusion.39), channel_id=1, source_target_pairs={{0,1},{1,2},{2,3},{3,4},{4,5},{5,6},{6,7},{7,8},{8,9},{9,10},{10,1... | collective-permute-start | bytes 147464 | tf_op jit(solution)/shard_map/ppermute | solution.py:26
  237.0 24.2 %collective-permute-start.18 = (f32[6,1,32,512]{3,2,1,0:T(8,128)S(1)}, f32[6,1,32,512]{3,2,1,0:T(8,128)S(1)}, u32[]{:S(2)}, u32[]{:S(2)}) collective-permute-start(f32[6,1,32,512]{3,2,1,0:T(8,128)S(1)} %get-tuple-element.47), channel_id=1, source_target_pairs={{1,0},{2,1},{3,2},{4,3},{5,4},{6,5},{7,6},{8,7},{9,8},{10,9},{11,1... | collective-permute-start | bytes 1179656 | tf_op jit(solution)/shard_map/ppermute | solution.py:29
  238.3 22.9 %collective-permute-start.19 = (f32[6,1,32,512]{3,2,1,0:T(8,128)S(1)}, f32[6,1,32,512]{3,2,1,0:T(8,128)S(1)}, u32[]{:S(2)}, u32[]{:S(2)}) collective-permute-start(f32[6,1,32,512]{3,2,1,0:T(8,128)S(1)} %get-tuple-element.46), channel_id=1, source_target_pairs={{0,1},{1,2},{2,3},{3,4},{4,5},{5,6},{6,7},{7,8},{8,9},{9,10},{10,1... | collective-permute-start | bytes 1179656 | tf_op jit(solution)/shard_map/ppermute | solution.py:26
  244.4 7.4 %collective-permute-start.32 = (f32[3,1,16,256]{3,2,1,0:T(8,128)S(1)}, f32[3,1,16,256]{3,2,1,0:T(8,128)S(1)}, u32[]{:S(2)}, u32[]{:S(2)}) collective-permute-start(f32[3,1,16,256]{3,2,1,0:T(8,128)S(1)} %fusion.37), channel_id=1, source_target_pairs={{1,0},{2,1},{3,2},{4,3},{5,4},{6,5},{7,6},{8,7},{9,8},{10,9},{11,1... | collective-permute-start | bytes 147464 | tf_op jit(solution)/shard_map/ppermute | solution.py:29
  245.7 6.9 %collective-permute-start.33 = (f32[3,1,16,256]{3,2,1,0:T(8,128)S(1)}, f32[3,1,16,256]{3,2,1,0:T(8,128)S(1)}, u32[]{:S(2)}, u32[]{:S(2)}) collective-permute-start(f32[3,1,16,256]{3,2,1,0:T(8,128)S(1)} %fusion.37), channel_id=1, source_target_pairs={{0,1},{1,2},{2,3},{3,4},{4,5},{5,6},{6,7},{7,8},{8,9},{9,10},{10,1... | collective-permute-start | bytes 147464 | tf_op jit(solution)/shard_map/ppermute | solution.py:26
  252.9 11.2 %collective-permute-start.34 = (f32[3,1,16,256]{3,2,1,0:T(8,128)S(1)}, f32[3,1,16,256]{3,2,1,0:T(8,128)S(1)}, u32[]{:S(2)}, u32[]{:S(2)}) collective-permute-start(f32[3,1,16,256]{3,2,1,0:T(8,128)S(1)} %fusion.35), channel_id=1, source_target_pairs={{1,0},{2,1},{3,2},{4,3},{5,4},{6,5},{7,6},{8,7},{9,8},{10,9},{11,1... | collective-permute-start | bytes 147464 | tf_op jit(solution)/shard_map/ppermute | solution.py:29
  254.2 9.9 %collective-permute-start.35 = (f32[3,1,16,256]{3,2,1,0:T(8,128)S(1)}, f32[3,1,16,256]{3,2,1,0:T(8,128)S(1)}, u32[]{:S(2)}, u32[]{:S(2)}) collective-permute-start(f32[3,1,16,256]{3,2,1,0:T(8,128)S(1)} %fusion.35), channel_id=1, source_target_pairs={{0,1},{1,2},{2,3},{3,4},{4,5},{5,6},{6,7},{7,8},{8,9},{9,10},{10,1... | collective-permute-start | bytes 147464 | tf_op jit(solution)/shard_map/ppermute | solution.py:26
  296.5 15.8 %all-to-all-start.3 = ((f32[16,1,768]{2,1,0:T(1,128)}), f32[16,1,768]{2,1,0:T(1,128)}, u32[]{:S(2)}, u32[]{:S(2)}) async-start(f32[16,1,768]{2,1,0:T(1,128)} %reshape.396), calls=%async_computation.3 | async-start | bytes 98304 | tf_op jit(solution)/shard_map/all_to_all | solution.py:178
  (59 other events, 543.2 us)
where the time goes:
time: 318 us; the launch traced here: 316 us
  starting transfers between devices  146 us (46%)
  local copies, waits for them, and re-layouts  102 us (32%)
  other arithmetic  52.2 us (16%)
  waiting for transfers between devices  13.8 us (4%)
    ppermute x18, starting transfers between devices, extended(): lax.ppermute(lax.slice_in_dim(block, block.shape[dim] - width, None, axis...  91.7 us
    broadcast_in_dim x12, local copies, waits for them, and re-layouts, prolong(): jnp.broadcast_to(block[:, :, None, :, None, :, None], (comps, depth, 2, r...  46.2 us
    reduce_sum x4, local copies, waits for them, and re-layouts, reduce_onto_parent(): return jnp.mean(shaped, axis=(2, 4, 6))  39 us
    ppermute x18, starting transfers between devices, extended(): lax.ppermute(lax.slice_in_dim(block, 0, width, axis=dim), axis, backward)  23.5 us
    reduce_sum x7, other arithmetic, reduce_onto_parent(): return jnp.mean(shaped, axis=(2, 4, 6))  18.3 us
    unnamed x98, local copies, waits for them, and re-layouts  10.5 us
    all_to_all x1, starting transfers between devices, on_device(): lax.all_to_all(jnp.transpose(potential, (0, 3, 2, 1)), 'slab', split_axis...  8.93 us
    ppermute x18, waiting for transfers between devices, extended(): lax.ppermute(lax.slice_in_dim(block, block.shape[dim] - width, None, axis...  8.3 us
  transfers between devices with their start and end apart: 40, of which 12 were waited for; matrix products, arithmetic and copies ran while one was open for 35% of the time, Pallas kernels for 0%

commit v1 on v0

--- a/solution.py
+++ b/solution.py
@@ -1,6 +1,10 @@
+import functools
+
 import jax
 import jax.numpy as jnp
 from jax import lax
+from jax.experimental import pallas as pl
+from jax.experimental.pallas import tpu as pltpu
 from jax.sharding import PartitionSpec as P
 
 STEPS = 2
@@ -150,7 +154,7 @@
     return jnp.concatenate([reduce_onto_parent(induction_tables[:3]), conduct[None]], 0)
 
 
-def on_device(
+def layered_on_device(
     melt_speeds,
     heat_state,
     eddy_quantities,
@@ -179,6 +183,623 @@
         jnp.transpose(potential, (0, 3, 2, 1)), "slab", split_axis=1, concat_axis=3, tiled=True
     )
     return (induction_tables[:3], induction_tables[3], induction_tables[4:], potential)
+
+
+ROW = 8
+LANES = 128
+MESH = pl.DeviceIdType.MESH
+
+
+def iota(shape, dim):
+    return lax.broadcasted_iota(jnp.int32, shape, dim)
+
+
+def thirds(value):
+    high = value.astype(jnp.bfloat16)
+    rest = value - high.astype(jnp.float32)
+    middle = rest.astype(jnp.bfloat16)
+    low = (rest - middle.astype(jnp.float32)).astype(jnp.bfloat16)
+    return high, middle, low
+
+
+def times_right(value, matrix):
+    rows = value.shape[0]
+    out = jnp.dot(
+        jnp.concatenate(thirds(value), 0), matrix, preferred_element_type=jnp.float32
+    )
+    return out[:rows] + out[rows : 2 * rows] + out[2 * rows :]
+
+
+def times_left(matrix, value):
+    return jnp.dot(
+        jnp.concatenate([matrix] * 3, 1),
+        jnp.concatenate(thirds(value), 0),
+        preferred_element_type=jnp.float32,
+    )
+
+
+def pairing(shape, fine_dim, scale):
+    fine = lax.shift_right_logical(iota(shape, fine_dim), 1)
+    return jnp.where(fine == iota(shape, 1 - fine_dim), scale, 0.0).astype(jnp.bfloat16)
+
+
+def left_roll(value, shift):
+    width = value.shape[-1]
+    shift = shift % width
+    return value if shift == 0 else pltpu.roll(value, width - shift, value.ndim - 1)
+
+
+def fused_kernel(
+    n,
+    xl,
+    melt_ref,
+    heat_ref,
+    eddy_ref,
+    zone_ref,
+    table_ref,
+    own_ref,
+    vel_out,
+    temp_out,
+    turb_out,
+    pot_out,
+    fields0,
+    fields1,
+    send_f,
+    recv_f,
+    send_b,
+    recv_b,
+    halo_out0,
+    halo_in0,
+    halo_out1,
+    halo_in1,
+    pot_a,
+    pot_b,
+    field1,
+    field2,
+    coil,
+    emf,
+    source,
+    inverse,
+    loads,
+    zone_sigma,
+    load_sem,
+    f_send_sem,
+    f_recv_sem,
+    b_send_sem,
+    b_recv_sem,
+    p_send_sem,
+    p_recv_sem,
+    h_send_sem,
+    h_recv_sem,
+):
+    me = lax.axis_index("slab")
+    fields = (fields0, fields1)
+    halo_out = (halo_out0, halo_out1)
+    halo_in = (halo_in0, halo_in1)
+    win = xl + 2 * SWEEPS
+    depth, rows = own_ref.shape[1:3]
+    fine_rows, width = heat_ref.shape[1:]
+    body = pl.ds(ROW, fine_rows)
+    cols = width // 2
+    lane = iota((rows, LANES), 1)
+    group = lane // win
+    inner = lane % win
+    sub = iota((rows, LANES), 0)
+
+    def peer(index):
+        return {"slab": index}
+
+    fetches = [
+        pltpu.make_async_copy(melt_ref, fields0.at[0:3, 1:3, body, :], load_sem.at[0]),
+        pltpu.make_async_copy(heat_ref, fields0.at[3, 1:3, body, :], load_sem.at[1]),
+        pltpu.make_async_copy(eddy_ref, fields0.at[4:6, 1:3, body, :], load_sem.at[2]),
+    ]
+    for fetch in fetches:
+        fetch.start()
+
+    barrier = pltpu.get_barrier_semaphore()
+    for offset in range(1, n):
+        pl.semaphore_signal(
+            barrier, inc=1, device_id=peer(lax.rem(me + offset, n)), device_id_type=MESH
+        )
+
+    for block in fields:
+        edge = jnp.zeros((6, 4, ROW, width), jnp.float32)
+        block[:, :, 0:ROW, :] = edge
+        block[:, :, ROW + fine_rows :, :] = edge
+
+    @pl.when(me == 0)
+    def _():
+        for block in fields:
+            block[:, 0, body, :] = jnp.zeros((6, fine_rows, width), jnp.float32)
+        for block in halo_in:
+            block[0] = jnp.zeros(block.shape[1:], jnp.float32)
+
+    @pl.when(me == n - 1)
+    def _():
+        for block in fields:
+            block[:, 3, body, :] = jnp.zeros((6, fine_rows, width), jnp.float32)
+        for block in halo_in:
+            block[1] = jnp.zeros(block.shape[1:], jnp.float32)
+
+    labels = zone_ref[0]
+    sigma0 = jnp.zeros(labels.shape, jnp.float32)
+    for region in range(table_ref.shape[0]):
+        sigma0 = sigma0 + jnp.where(labels == region, table_ref[region], 0.0)
+    zone_sigma[...] = sigma0
+
+    slot = inner // SWEEPS
+    for z in range(depth):
+        to_left = jnp.zeros((rows, LANES), jnp.float32)
+        to_right = to_left
+        for a in range(3):
+            value = own_ref[a, z]
+            to_left = jnp.where(slot == a, left_roll(value, SWEEPS - SWEEPS * a), to_left)
+            to_right = jnp.where(slot == a, left_roll(value, xl - SWEEPS * a), to_right)
+        halo_out0[0, z] = to_left
+        halo_out0[1, z] = to_right
+
+    def plane_copies(step):
+        block = fields[step]
+        down = pltpu.make_async_remote_copy(
+            src_ref=block.at[:, 1, body, :],
+            dst_ref=block.at[:, 3, body, :],
+            send_sem=p_send_sem.at[step, 0],
+            recv_sem=p_recv_sem.at[step, 0],
+            device_id=peer(me - 1),
+            device_id_type=MESH,
+        )
+        up = pltpu.make_async_remote_copy(
+            src_ref=block.at[:, 2, body, :],
+            dst_ref=block.at[:, 0, body, :],
+            send_sem=p_send_sem.at[step, 1],
+            recv_sem=p_recv_sem.at[step, 1],
+            device_id=peer(me + 1),
+            device_id_type=MESH,
+        )
+        return down, up
+
+    def halo_copies(step):
+        down = pltpu.make_async_remote_copy(
+            src_ref=halo_out[step].at[0],
+            dst_ref=halo_in[step].at[1],
+            send_sem=h_send_sem.at[step, 0],
+            recv_sem=h_recv_sem.at[step, 0],
+            device_id=peer(me - 1),
+            device_id_type=MESH,
+        )
+        up = pltpu.make_async_remote_copy(
+            src_ref=halo_out[step].at[1],
+            dst_ref=halo_in[step].at[0],
+            send_sem=h_send_sem.at[step, 1],
+            recv_sem=h_recv_sem.at[step, 1],
+            device_id=peer(me + 1),
+            device_id_type=MESH,
+        )
+        return down, up
+
+    def start_pair(pair):
+        @pl.when(me > 0)
+        def _():
+            pair[0].start()
+
+        @pl.when(me < n - 1)
+        def _():
+            pair[1].start()
+
+    def receive_pair(pair):
+        @pl.when(me < n - 1)
+        def _():
+            pair[0].wait_recv()
+
+        @pl.when(me > 0)
+        def _():
+            pair[1].wait_recv()
+
+    def sent_pair(pair):
+        @pl.when(me > 0)
+        def _():
+            pair[0].wait_send()
+
+        @pl.when(me < n - 1)
+        def _():
+            pair[1].wait_send()
+
+    def spread(step, send, recv, send_sem, recv_sem):
+        copies = []
+        for offset in range(1, n):
+            target = lax.rem(me + offset, n)
+            copies.append(
+                pltpu.make_async_remote_copy(
+                    src_ref=send.at[step, target],
+                    dst_ref=recv.at[step, me],
+                    send_sem=send_sem.at[step, offset],
+                    recv_sem=recv_sem.at[step, offset],
+                    device_id=peer(target),
+                    device_id_type=MESH,
+                )
+            )
+        return copies
+
+    halve_rows = pairing((4 * rows, 4 * fine_rows), 1, 0.125)
+    halve_cols = pairing((2 * LANES, LANES), 0, 1.0)
+    double_rows = pairing((4 * fine_rows, 4 * rows), 0, 1.0)
+    double_cols = pairing((LANES, 2 * LANES), 1, 1.0)
+
+    def restrict_and_window(step):
+        block = fields[step]
+        parts = [block[f, 1, body, :] + block[f, 2, body, :] for f in range(3)]
+        parts.append(
+            jnp.exp(-thermal_gradient_factor * block[3, 1, body, :])
+            + jnp.exp(-thermal_gradient_factor * block[3, 2, body, :])
+        )
+        short = times_left(halve_rows, jnp.concatenate(parts, 0))
+        coarse = jnp.concatenate(
+            [
+                times_right(short[:, at : at + 2 * LANES], halve_cols)
+                for at in range(0, width, 2 * LANES)
+            ],
+            1,
+        )
+        comps = [coarse[c * rows : (c + 1) * rows] for c in range(4)]
+        comps[3] = comps[3] * zone_sigma[...]
+        for target in range(n):
+            first = target * xl - SWEEPS
+            message = jnp.zeros((rows, LANES), jnp.float32)
+            for c in range(4):
+                moved = left_roll(comps[c], first - c * win)[:, :LANES]
+                message = jnp.where(group == c, moved, message)
+            send_f[step, target] = message
+
+    def turned(value):
+        return left_roll(value, win), left_roll(value, 2 * win), left_roll(value, 3 * win)
+
+    def relax_all(step):
+        x_at = me * xl - SWEEPS + inner
+        valid = (x_at >= 0) & (x_at < cols) & (group < 3)
+
+        def prepare(z, carry):
+            value = recv_f[step, z]
+            one, two, three = turned(value)
+            next_comp = jnp.where(group < 2, one, two)
+            last_comp = jnp.where(group == 0, two, three)
+            sigma = jnp.where(group == 0, three, jnp.where(group == 1, two, one))
+            motional = next_comp * field2[z] - last_comp * field1[z]
+            emf[z] = motional
+            source[z] = sigma * motional + coil[z]
+            inverse[z] = jnp.where(valid, 1.0 / (6.0 + coupling * sigma), 0.0)
+            return carry
+
+        lax.fori_loop(0, depth, prepare, 0)
+
+        def sweep(old, new):
+            for z in range(depth):
+                centre = old[z + 1]
+                total = source[z] + old[z] + old[z + 2]
+                total = total + left_roll(centre, 1) + left_roll(centre, LANES - 1)
+                total = total + jnp.where(sub == 0, 0.0, pltpu.roll(centre, 1, 0))
+                total = total + jnp.where(sub == rows - 1, 0.0, pltpu.roll(centre, rows - 1, 0))
+                new[z + 1] = total * inverse[z]
+
+        def two_sweeps(index, carry):
+            sweep(pot_a, pot_b)
+            sweep(pot_b, pot_a)
+            return carry
+
+        lax.fori_loop(0, SWEEPS // 2, two_sweeps, 0)
+
+        half = rows // 2
+        packed = iota((half, LANES), 1) // xl
+
+        def load(z, carry):
+            value = recv_f[step, z]
+            one, two, three = turned(value)
+            sigma = jnp.where(group == 0, three, jnp.where(group == 1, two, one))
+            drive = emf[z] - coupling * pot_a[z + 1]
+            current = sigma * drive + coil[z]
+            one, two, three = turned(current)
+            next_comp = jnp.where(group < 2, one, two)
+            last_comp = jnp.where(group == 0, two, three)
+            force = next_comp * field2[z] - last_comp * field1[z]
+            one, two, three = turned(drive * drive)
+            both = jnp.where(group == 3, value * (one + two + three), force)
+            message = jnp.zeros((half, LANES), jnp.float32)
+            for h in range(2):
+                piece = both[h * half : (h + 1) * half]
+                for c in range(4):
+                    at = 4 * h + c
+                    moved = left_roll(piece, c * win + SWEEPS - at * xl)
+                    message = jnp.where(packed == at, moved, message)
+            send_b[step, z] = message
+            return carry
+
+        lax.fori_loop(0, depth, load, 0)
+
+    def prolong_loads(step):
+        half = rows // 2
+        packed = iota((half, LANES), 1) // xl
+        per = LANES // xl
+        strips = []
+        for c in range(4):
+            for h in range(2):
+                strip = []
+                for first in range(0, n, per):
+                    piece = jnp.zeros((half, LANES), jnp.float32)
+                    for d in range(per):
+                        moved = left_roll(recv_b[step, first + d], (4 * h + c - d) * xl)
+                        piece = jnp.where(packed == d, moved, piece)
+                    strip.append(piece)
+                strips.append(jnp.concatenate(strip, 1))
+        coarse = jnp.concatenate(strips, 0)
+        wide = jnp.concatenate(
+            [
+                times_right(coarse[:, at : at + LANES], double_cols)
+                for at in range(0, cols, LANES)
+            ],
+            1,
+        )
+        loads[...] = times_left(double_rows, wide)
+
+    def advance_all(step, store):
+        block = fields[step]
+        sub8 = iota((ROW, width), 0)
+        lane8 = iota((ROW, width), 1)
+
+        def chunk(plane, index, carry):
+            low = pl.multiple_of(index * ROW, ROW)
+            at = pl.multiple_of(index * ROW + ROW, ROW)
+            high = pl.multiple_of(index * ROW + 2 * ROW, ROW)
+            here = pl.ds(at, ROW)
+            centre = [block[f, plane, here, :] for f in range(6)]
+            kinetic, dissip = centre[4], centre[5]
+            eddy = eddy_coeff * kinetic * kinetic / jnp.maximum(dissip, turb_floor)
+            diffuse = molecular + eddy
+            strain = None
+            for f in range(6):
+                mid = centre[f]
+                z_minus = block[f, plane - 1, here, :]
+                z_plus = block[f, plane + 1, here, :]
+                before = block[f, plane, pl.ds(low, ROW), :]
+                after = block[f, plane, pl.ds(high, ROW), :]
+                y_minus = pltpu.roll(jnp.where(sub8 == ROW - 1, before, mid), 1, 0)
+                y_plus = pltpu.roll(jnp.where(sub8 == 0, after, mid), ROW - 1, 0)
+                x_minus = jnp.where(lane8 == 0, 0.0, pltpu.roll(mid, 1, 1))
+                x_plus = jnp.where(lane8 == width - 1, 0.0, pltpu.roll(mid, width - 1, 1))
+                laplace = (
+                    (z_plus + z_minus) + (y_plus + y_minus) + (x_plus + x_minus) - 6.0 * mid
+                )
+                grad_z = 0.5 * (z_plus - z_minus)
+                grad_y = 0.5 * (y_plus - y_minus)
+                grad_x = 0.5 * (x_plus - x_minus)
+                transport = centre[0] * grad_x + centre[1] * grad_y + centre[2] * grad_z
+                if f < 3:
+                    square = grad_x * grad_x + grad_y * grad_y + grad_z * grad_z
+                    strain = square if strain is None else strain + square
+                if f < 4:
+                    src = loads[pl.ds(pl.multiple_of(f * fine_rows + index * ROW, ROW), ROW), :]
+                elif f == 4:
+                    produce = eddy * strain
+                    src = produce - dissip
+                else:
+                    src = (
+                        (prod_coeff * produce - dissip_coeff * dissip)
+                        * dissip
+                        / jnp.maximum(kinetic, turb_floor)
+                    )
+                if f == 3:
+                    spread_by = heat_diffuse + eddy * (1.0 / 0.9)
+                elif f == 5:
+                    spread_by = molecular + eddy * (1.0 / 1.3)
+                else:
+                    spread_by = diffuse
+                store(
+                    f, plane, index, mid + time_step * (spread_by * laplace - transport + src)
+                )
+            return carry
+
+        for plane in (1, 2):
+            lax.fori_loop(0, fine_rows // ROW, functools.partial(chunk, plane), 0)
+
+    def store_mid(f, plane, index, value):
+        fields1[f, plane, pl.ds(pl.multiple_of(index * ROW + ROW, ROW), ROW), :] = value
+
+    def store_last(f, plane, index, value):
+        here = pl.ds(pl.multiple_of(index * ROW, ROW), ROW)
+        if f < 3:
+            vel_out[f, plane - 1, here, :] = value
+        elif f == 3:
+            temp_out[plane - 1, here, :] = value
+        else:
+            turb_out[f - 4, plane - 1, here, :] = value
+
+    pack = win // SWEEPS
+
+    def pack_potential():
+        for z in range(0, depth, pack):
+            to_left = jnp.zeros((rows, LANES), jnp.float32)
+            to_right = to_left
+            for k in range(pack):
+                value = pot_a[z + k + 1]
+                to_left = jnp.where(slot == k, left_roll(value, SWEEPS - SWEEPS * k), to_left)
+                to_right = jnp.where(slot == k, left_roll(value, xl - SWEEPS * k), to_right)
+            halo_out1[0, z // pack] = to_left
+            halo_out1[1, z // pack] = to_right
+
+    def framed(own, from_left, from_right, k):
+        left = left_roll(from_left, SWEEPS * k)
+        right = left_roll(from_right, SWEEPS * k - (win - SWEEPS))
+        whole = jnp.where(
+            inner < SWEEPS, left, jnp.where(inner >= win - SWEEPS, right, own)
+        )
+        return jnp.where(group < 3, whole, 0.0)
+
+    for step in range(STEPS):
+        if step == 0:
+            for fetch in fetches:
+                fetch.wait()
+        restrict_and_window(step)
+        if step == 0:
+            pl.semaphore_wait(barrier, n - 1)
+        forward = spread(step, send_f, recv_f, f_send_sem, f_recv_sem)
+        for copy in forward:
+            copy.start()
+        if step == 0:
+            halos = halo_copies(0)
+            start_pair(halos)
+        planes = plane_copies(step)
+        start_pair(planes)
+        recv_f[step, me] = send_f[step, me]
+        if step == 0:
+            pot_a[0] = jnp.zeros((rows, LANES), jnp.float32)
+            pot_a[depth + 1] = jnp.zeros((rows, LANES), jnp.float32)
+            pot_b[0] = jnp.zeros((rows, LANES), jnp.float32)
+            pot_b[depth + 1] = jnp.zeros((rows, LANES), jnp.float32)
+        receive_pair(halos)
+        if step == 0:
+            for z in range(depth):
+                sides = halo_in0[0, z], halo_in0[1, z]
+                pot_a[z + 1] = framed(own_ref[0, z], *sides, 0)
+                one, two, three = turned(framed(own_ref[1, z], *sides, 1))
+                field1[z] = jnp.where(group < 2, one, two)
+                field2[z] = jnp.where(group == 0, two, three)
+                coil[z] = framed(own_ref[2, z], *sides, 2)
+        else:
+            for z in range(depth):
+                sides = halo_in1[0, z // pack], halo_in1[1, z // pack]
+                pot_a[z + 1] = framed(pot_a[z + 1], *sides, z % pack)
+        sent_pair(halos)
+        for copy in forward:
+            copy.wait_recv()
+        relax_all(step)
+        back = spread(step, send_b, recv_b, b_send_sem, b_recv_sem)
+        for copy in back:
+            copy.start()
+        recv_b[step, me] = send_b[step, me]
+        if step == 0:
+            pack_potential()
+            halos = halo_copies(1)
+            start_pair(halos)
+        else:
+            pot_out[...] = pot_a[1 : depth + 1]
+        for copy in forward:
+            copy.wait_send()
+        for copy in back:
+            copy.wait_recv()
+        prolong_loads(step)
+        receive_pair(planes)
+        advance_all(step, store_mid if step == 0 else store_last)
+        for copy in back:
+            copy.wait_send()
+        sent_pair(planes)
+
+
+def fused_on_device(
+    melt_speeds,
+    heat_state,
+    eddy_quantities,
+    zone_labels,
+    zone_resistivity_inverse,
+    imposed_induction,
+    winding_current,
+    window_entry_induction_guess,
+):
+    n = lax.axis_size("slab")
+    _, xl, rows, depth = imposed_induction.shape
+    _, fine_rows, width = heat_state.shape
+    win = xl + 2 * SWEEPS
+    own = jnp.stack([window_entry_induction_guess, imposed_induction, winding_current])
+    own = jnp.transpose(own, (0, 4, 3, 1, 2))
+    own = jnp.pad(own, ((0, 0), (0, 0), (0, 0), (0, 1), (SWEEPS, SWEEPS)))
+    own = own.reshape(3, depth, rows, 4 * win)
+
+    def vmem(*shape):
+        return pltpu.VMEM(shape, jnp.float32)
+
+    plane = (depth, rows, LANES)
+    dma = pltpu.SemaphoreType.DMA
+    whole = pl.BlockSpec(memory_space=pltpu.VMEM)
+    anywhere = pl.BlockSpec(memory_space=pl.ANY)
+    vel, temp, turb, pot = pl.pallas_call(
+        functools.partial(fused_kernel, n, xl),
+        out_shape=(
+            jax.ShapeDtypeStruct(melt_speeds.shape, jnp.float32),
+            jax.ShapeDtypeStruct(heat_state.shape, jnp.float32),
+            jax.ShapeDtypeStruct(eddy_quantities.shape, jnp.float32),
+            jax.ShapeDtypeStruct(plane, jnp.float32),
+        ),
+        in_specs=[
+            anywhere,
+            anywhere,
+            anywhere,
+            whole,
+            pl.BlockSpec(memory_space=pltpu.SMEM),
+            whole,
+        ],
+        out_specs=(whole,) * 4,
+        scratch_shapes=[
+            vmem(6, 4, fine_rows + 2 * ROW, width),
+            vmem(6, 4, fine_rows + 2 * ROW, width),
+            vmem(STEPS, n, rows, LANES),
+            vmem(STEPS, n, rows, LANES),
+            vmem(STEPS, n, rows // 2, LANES),
+            vmem(STEPS, n, rows // 2, LANES),
+            vmem(2, *plane),
+            vmem(2, *plane),
+            vmem(2, depth * SWEEPS // win, rows, LANES),
+            vmem(2, depth * SWEEPS // win, rows, LANES),
+            vmem(depth + 2, rows, LANES),
+            vmem(depth + 2, rows, LANES),
+            vmem(*plane),
+            vmem(*plane),
+            vmem(*plane),
+            vmem(*plane),
+            vmem(*plane),
+            vmem(*plane),
+            vmem(4 * fine_rows, width),
+            vmem(rows, width // 2),
+            dma((3,)),
+            dma((STEPS, n)),
+            dma((STEPS, n)),
+            dma((STEPS, n)),
+            dma((STEPS, n)),
+            dma((STEPS, 2)),
+            dma((STEPS, 2)),
+            dma((STEPS, 2)),
+            dma((STEPS, 2)),
+        ],
+        compiler_params=pltpu.CompilerParams(
+            collective_id=0, has_side_effects=True, vmem_limit_bytes=40 * 1024 * 1024
+        ),
+    )(melt_speeds, heat_state, eddy_quantities, zone_labels, zone_resistivity_inverse, own)
+    pot = pot.reshape(depth, rows, 4, win)[:, :, :3, SWEEPS : SWEEPS + xl]
+    return vel, temp, turb, jnp.transpose(pot, (2, 3, 1, 0))
+
+
+def fits_fused(n, heat_state, imposed_induction):
+    _, xl, rows, depth = imposed_induction.shape
+    planes, fine_rows, width = heat_state.shape
+    win = xl + 2 * SWEEPS
+    return (
+        STEPS == 2
+        and SWEEPS % 2 == 0
+        and n > 1
+        and planes == 2
+        and depth == n
+        and rows == 2 * ROW
+        and fine_rows == 2 * rows
+        and width == 2 * n * xl
+        and width % (4 * LANES) == 0
+        and 4 * win == LANES
+        and xl == 2 * SWEEPS
+        and n % (LANES // xl) == 0
+        and depth % (win // SWEEPS) == 0
+    )
+
+
+def on_device(*args):
+    if fits_fused(lax.axis_size("slab"), args[1], args[5]):
+        return fused_on_device(*args)
+    return layered_on_device(*args)
 
 
 def solution(mesh):

time: 318 us -> 57.7 us (0.18)
  starting transfers between devices: 146 us -> 0 us
  local copies, waits for them, and re-layouts: 102 us -> 7.78 us
  other arithmetic: 52.2 us -> 1.36 us
  Pallas kernels: 0 us -> 47.7 us
  waiting for transfers between devices: 13.8 us -> 0 us
    ppermute x36 -> x0, starting transfers between devices: 115 us -> none  [the longest x18 91.7 us: extended(): lax.ppermute(lax.slice_in_dim(block, block.shape[dim] - width, None, axis...]
    pallas_call x0 -> x1, Pallas kernels: none -> 47.7 us  [fused_on_device(): pl.pallas_call(functools.partial(fused_kernel, n, xl), out_shape=(jax.Sha...]
    broadcast_in_dim x12 -> x0, local copies, waits for them, and re-layouts: 46.2 us -> none  [prolong(): jnp.broadcast_to(block[:, :, None, :, None, :, None], (comps, depth, 2, r...]
    reduce_sum x4 -> x0, local copies, waits for them, and re-layouts: 39 us -> none  [reduce_onto_parent(): return jnp.mean(shaped, axis=(2, 4, 6))]
    all_to_all x4 -> x0, starting transfers between devices: 30.3 us -> none  [the longest x1 8.93 us: on_device(): lax.all_to_all(jnp.transpose(potential, (0, 3, 2, 1)), 'slab', split_axis...]
    reduce_sum x12 -> x0, other arithmetic: 20.3 us -> none  [the longest x7 18.3 us: reduce_onto_parent(): return jnp.mean(shaped, axis=(2, 4, 6))]
    unnamed x98 -> x13, local copies, waits for them, and re-layouts: 10.5 us -> 2.12 us
    ppermute x36 -> x0, waiting for transfers between devices: 8.34 us -> none  [the longest x18 8.3 us: extended(): lax.ppermute(lax.slice_in_dim(block, block.shape[dim] - width, None, axis...]
  transfers between devices with their start and end apart: 40 -> 0, of which waited for: 12 -> 0; matrix products, arithmetic and copies ran while one was open for 35% -> 0% of each run, Pallas kernels for 0% -> 0%
where the time goes in v1:
time: 57.7 us; the launch traced here: 57.6 us
  Pallas kernels  47.7 us (83%)
  local copies, waits for them, and re-layouts  7.78 us (13%)
  other arithmetic  1.36 us (2%)
  between operations  0.71 us (1%)
    pallas_call x1, Pallas kernels, fused_on_device(): pl.pallas_call(functools.partial(fused_kernel, n, xl), out_shape=(jax.Sha...  47.7 us
    reshape x1, local copies, waits for them, and re-layouts, fused_on_device(): own = own.reshape(3, depth, rows, 4 * win)  2.4 us
    unnamed x13, local copies, waits for them, and re-layouts  2.12 us
    pad x1, local copies, waits for them, and re-layouts, fused_on_device(): own = jnp.pad(own, ((0, 0), (0, 0), (0, 0), (0, 1), (SWEEPS, SWEEPS)))  1.98 us
    transpose x1, other arithmetic, fused_on_device(): own = jnp.transpose(own, (0, 4, 3, 1, 2))  1.36 us

profile of v1, /device:TPU:0, one launch (start us, length us, event | category | flops | bytes accessed | tf_op | source)
XLA Modules:
  0.0 57.6 jit_solution(2661499935090735253)
XLA Ops:
  0.6 1.4 %maximum_bitcast_fusion = f32[3,16,16,3,16]{1,2,4,3,0:T(8,128)S(1)} fusion(f32[1,3,16,16,16]{4,3,2,1,0:T(8,128)} %bitcast.11, f32[1,3,16,16,16]{4,3,2,1,0:T(8,128)} %bitcast.12, f32[1,3,16,16,16]{4,3,2,1,0:T(8,128)} %bitcast.13), kind=kLoop, calls=%fused_computation | loop fusion | flops 73728 | bytes 294912 | tf_op jit(solution)/shard_map/transpose | solution.py:711
  2.0 2.0 %pad.4 = f32[3,16,16,4,32]{1,2,4,3,0:T(8,128)} pad(f32[3,16,16,3,16]{1,2,4,3,0:T(8,128)S(1)} %maximum_bitcast_fusion, f32[]{:T(128)} %constant.2.clone.1), padding=0_0x0_0x0_0x0_1x8_8 | pad | bytes 540676 | tf_op jit(solution)/shard_map/jit(_pad)/pad | solution.py:712
  4.0 0.0 copy-start
  4.0 0.0 copy-start.1
  4.0 0.0 copy-start.2
  4.0 0.0 copy-start.3
  4.0 0.0 copy-start.4
  4.0 2.4 %copy.14.own_ref = f32[3,16,16,128]{3,2,1,0:T(8,128)S(1)} copy(f32[3,16,16,128]{1,2,3,0:T(8,128)} %bitcast.9) | data formatting | bytes 786432 | tf_op jit(solution)/shard_map/reshape | solution.py:713
  6.4 0.0 copy-done
  6.4 0.0 copy-done.1
  6.4 0.0 copy-done.2
  6.4 0.0 copy-done.3
  6.4 0.0 copy-done.4
  6.5 47.7 %shard_map.111 = (f32[3,2,32,512]{3,2,1,0:T(8,128)S(1)}, f32[2,32,512]{2,1,0:T(8,128)S(1)}, f32[2,2,32,512]{3,2,1,0:T(8,128)S(1)}, f32[16,16,128]{2,1,0:T(8,128)S(1)}) custom-call(f32[3,2,32,512]{3,2,1,0:T(8,128)S(1)} %copy-done, f32[2,32,512]{2,1,0:T(8,128)S(1)} %copy-done.2, f32[2,2,32,512]{3,2,1,0:T(8,128)S(1)} %copy-done.1, s32[1,16,256]{2,1,0:T(8,128)S(1)} %copy-done.3, ...), custom_call_target="tpu_custom_call" | custom-call | tf_op jit(solution)/shard_map/pallas_call | solution.py:722
  54.2 0.5 copy.15
  54.7 0.8 %slice_bitcast_fusion = f32[3,16,16,16]{3,2,1,0:T(8,128)} fusion(f32[16,16,4,32]{0,1,3,2:T(8,128)S(1)} %bitcast.10), kind=kLoop, calls=%fused_computation.1 | loop fusion | bytes 98304 | tf_op jit(solution)/shard_map/transpose | solution.py:775
  55.5 0.7 %copy.19 = f32[3,2,32,512]{3,2,1,0:T(8,128)} copy(f32[3,2,32,512]{3,2,1,0:T(8,128)S(1)} %get-tuple-element.16) | data formatting | bytes 786432
  56.2 0.7 %copy.20 = f32[2,32,512]{2,1,0:T(8,128)} copy(f32[2,32,512]{2,1,0:T(8,128)S(1)} %get-tuple-element.17) | data formatting | bytes 262144
  56.9 0.7 %copy.21 = f32[2,2,32,512]{3,2,1,0:T(8,128)} copy(f32[2,2,32,512]{3,2,1,0:T(8,128)S(1)} %get-tuple-element.18) | data formatting | bytes 524288
Async XLA Ops:
  4.0 2.4 %copy-start = (f32[3,2,32,512]{3,2,1,0:T(8,128)S(1)}, f32[3,2,32,512]{3,2,1,0:T(8,128)}, u32[]{:S(2)}) copy-start(f32[3,2,32,512]{3,2,1,0:T(8,128)} %melt_ref.1) | copy-start | bytes 1179652
  4.0 2.4 %copy-start.1 = (f32[2,2,32,512]{3,2,1,0:T(8,128)S(1)}, f32[2,2,32,512]{3,2,1,0:T(8,128)}, u32[]{:S(2)}) copy-start(f32[2,2,32,512]{3,2,1,0:T(8,128)} %eddy_ref.1) | copy-start | bytes 786436
  4.0 2.4 %copy-start.2 = (f32[2,32,512]{2,1,0:T(8,128)S(1)}, f32[2,32,512]{2,1,0:T(8,128)}, u32[]{:S(2)}) copy-start(f32[2,32,512]{2,1,0:T(8,128)} %heat_ref.1) | copy-start | bytes 393220
  4.0 2.5 %copy-start.3 = (s32[1,16,256]{2,1,0:T(8,128)S(1)}, s32[1,16,256]{2,1,0:T(8,128)}, u32[]{:S(2)}) copy-start(s32[1,16,256]{2,1,0:T(8,128)} %zone_ref.1) | copy-start | bytes 49156
  4.0 2.5 %copy-start.4 = (f32[8]{0:T(128)S(1)}, f32[8]{0:T(128)}, u32[]{:S(2)}) copy-start(f32[8]{0:T(128)} %table_ref.1) | copy-start | bytes 100

commit v2 on v1

--- a/solution.py
+++ b/solution.py
@@ -237,7 +237,9 @@
     eddy_ref,
     zone_ref,
     table_ref,
-    own_ref,
+    guess_ref,
+    induction_ref,
+    winding_ref,
     vel_out,
     temp_out,
     turb_out,
@@ -248,6 +250,7 @@
     recv_f,
     send_b,
     recv_b,
+    own_ref,
     halo_out0,
     halo_in0,
     halo_out1,
@@ -277,7 +280,7 @@
     halo_out = (halo_out0, halo_out1)
     halo_in = (halo_in0, halo_in1)
     win = xl + 2 * SWEEPS
-    depth, rows = own_ref.shape[1:3]
+    depth, rows = guess_ref.shape[1:3]
     fine_rows, width = heat_ref.shape[1:]
     body = pl.ds(ROW, fine_rows)
     cols = width // 2
@@ -327,6 +330,24 @@
     for region in range(table_ref.shape[0]):
         sigma0 = sigma0 + jnp.where(labels == region, table_ref[region], 0.0)
     zone_sigma[...] = sigma0
+
+    def blank(lanes):
+        return jnp.zeros((rows, lanes), jnp.float32)
+
+    for a, coarse_ref in enumerate((guess_ref, induction_ref, winding_ref)):
+        for z in range(depth):
+            own_ref[a, z] = jnp.concatenate(
+                [
+                    blank(SWEEPS),
+                    coarse_ref[0, z],
+                    blank(2 * SWEEPS),
+                    coarse_ref[1, z],
+                    blank(2 * SWEEPS),
+                    coarse_ref[2, z],
+                    blank(SWEEPS + win),
+                ],
+                1,
+            )
 
     slot = inner // SWEEPS
     for z in range(depth):
@@ -458,7 +479,7 @@
         x_at = me * xl - SWEEPS + inner
         valid = (x_at >= 0) & (x_at < cols) & (group < 3)
 
-        def prepare(z, carry):
+        def prepare(z):
             value = recv_f[step, z]
             one, two, three = turned(value)
             next_comp = jnp.where(group < 2, one, two)
@@ -468,9 +489,9 @@
             emf[z] = motional
             source[z] = sigma * motional + coil[z]
             inverse[z] = jnp.where(valid, 1.0 / (6.0 + coupling * sigma), 0.0)
-            return carry
-
-        lax.fori_loop(0, depth, prepare, 0)
+
+        for z in range(depth):
+            prepare(z)
 
         def sweep(old, new):
             for z in range(depth):
@@ -491,7 +512,7 @@
         half = rows // 2
         packed = iota((half, LANES), 1) // xl
 
-        def load(z, carry):
+        def load(z):
             value = recv_f[step, z]
             one, two, three = turned(value)
             sigma = jnp.where(group == 0, three, jnp.where(group == 1, two, one))
@@ -511,9 +532,9 @@
                     moved = left_roll(piece, c * win + SWEEPS - at * xl)
                     message = jnp.where(packed == at, moved, message)
             send_b[step, z] = message
-            return carry
-
-        lax.fori_loop(0, depth, load, 0)
+
+        for z in range(depth):
+            load(z)
 
     def prolong_loads(step):
         half = rows // 2
@@ -680,7 +701,10 @@
             halos = halo_copies(1)
             start_pair(halos)
         else:
-            pot_out[...] = pot_a[1 : depth + 1]
+            for c in range(3):
+                for z in range(depth):
+                    at = c * win + SWEEPS
+                    pot_out[c, z] = pot_a[z + 1][:, at : at + xl]
         for copy in forward:
             copy.wait_send()
         for copy in back:
@@ -707,10 +731,10 @@
     _, xl, rows, depth = imposed_induction.shape
     _, fine_rows, width = heat_state.shape
     win = xl + 2 * SWEEPS
-    own = jnp.stack([window_entry_induction_guess, imposed_induction, winding_current])
-    own = jnp.transpose(own, (0, 4, 3, 1, 2))
-    own = jnp.pad(own, ((0, 0), (0, 0), (0, 0), (0, 1), (SWEEPS, SWEEPS)))
-    own = own.reshape(3, depth, rows, 4 * win)
+    coarse = [
+        jnp.transpose(value, (0, 3, 2, 1))
+        for value in (window_entry_induction_guess, imposed_induction, winding_current)
+    ]
 
     def vmem(*shape):
         return pltpu.VMEM(shape, jnp.float32)
@@ -725,7 +749,7 @@
             jax.ShapeDtypeStruct(melt_speeds.shape, jnp.float32),
             jax.ShapeDtypeStruct(heat_state.shape, jnp.float32),
             jax.ShapeDtypeStruct(eddy_quantities.shape, jnp.float32),
-            jax.ShapeDtypeStruct(plane, jnp.float32),
+            jax.ShapeDtypeStruct((3, depth, rows, xl), jnp.float32),
         ),
         in_specs=[
             anywhere,
@@ -733,6 +757,8 @@
             anywhere,
             whole,
             pl.BlockSpec(memory_space=pltpu.SMEM),
+            whole,
+            whole,
             whole,
         ],
         out_specs=(whole,) * 4,
@@ -743,6 +769,7 @@
             vmem(STEPS, n, rows, LANES),
             vmem(STEPS, n, rows // 2, LANES),
             vmem(STEPS, n, rows // 2, LANES),
+            vmem(3, *plane),
             vmem(2, *plane),
             vmem(2, *plane),
             vmem(2, depth * SWEEPS // win, rows, LANES),
@@ -770,9 +797,8 @@
         compiler_params=pltpu.CompilerParams(
             collective_id=0, has_side_effects=True, vmem_limit_bytes=40 * 1024 * 1024
         ),
-    )(melt_speeds, heat_state, eddy_quantities, zone_labels, zone_resistivity_inverse, own)
-    pot = pot.reshape(depth, rows, 4, win)[:, :, :3, SWEEPS : SWEEPS + xl]
-    return vel, temp, turb, jnp.transpose(pot, (2, 3, 1, 0))
+    )(melt_speeds, heat_state, eddy_quantities, zone_labels, zone_resistivity_inverse, *coarse)
+    return vel, temp, turb, jnp.transpose(pot, (0, 3, 2, 1))
 
 
 def fits_fused(n, heat_state, imposed_induction):

time: 57.7 us -> 48.2 us (0.84)
  Pallas kernels: 47.7 us -> 40.9 us
  other arithmetic: 1.36 us -> 0 us
  local copies, waits for them, and re-layouts: 7.78 us -> 6.46 us
    pallas_call x1, Pallas kernels: 47.7 us -> 40.9 us  [fused_on_device(): pl.pallas_call(functools.partial(fused_kernel, n, xl), out_shape=(jax.Sha...]
    unnamed x13 -> x21, local copies, waits for them, and re-layouts: 2.12 us -> 6.46 us
    reshape x2 -> x0, local copies, waits for them, and re-layouts: 2.9 us -> none  [the longest x1 2.4 us: fused_on_device(): own = own.reshape(3, depth, rows, 4 * win)]
    pad x1 -> x0, local copies, waits for them, and re-layouts: 1.98 us -> none  [fused_on_device(): own = jnp.pad(own, ((0, 0), (0, 0), (0, 0), (0, 1), (SWEEPS, SWEEPS)))]
    transpose x1 -> x0, other arithmetic: 1.36 us -> none  [fused_on_device(): own = jnp.transpose(own, (0, 4, 3, 1, 2))]
    transpose x1 -> x0, local copies, waits for them, and re-layouts: 0.78 us -> none  [fused_on_device(): return (vel, temp, turb, jnp.transpose(pot, (2, 3, 1, 0)))]
where the time goes in v2:
time: 48.2 us; the launch traced here: 48.1 us
  Pallas kernels  40.9 us (85%)
  local copies, waits for them, and re-layouts  6.46 us (13%)
  between operations  0.71 us (1%)
    pallas_call x1, Pallas kernels, fused_on_device(): pl.pallas_call(functools.partial(fused_kernel, n, xl), out_shape=(jax.Sha...  40.9 us
    unnamed x21, local copies, waits for them, and re-layouts  6.46 us

profile of v2, /device:TPU:0, one launch (start us, length us, event | category | flops | bytes accessed | tf_op | source)
XLA Modules:
  0.0 48.1 jit_solution(451365540841708938)
XLA Ops:
  0.6 0.0 copy-start.5
  0.6 1.3 %copy.13 = f32[3,16,16,16]{1,2,3,0:T(8,128)S(1)} copy(f32[3,16,16,16]{3,2,1,0:T(8,128)} %param.13) | data formatting | bytes 98304 | tf_op args[5]
  1.9 0.0 copy-done.5
  2.0 0.0 copy-start.6
  2.0 0.0 copy-start.3
  2.0 0.3 copy.14
  2.3 0.7 %copy-done.6 = f32[3,16,16,16]{3,2,1,0:T(8,128)S(1)} copy-done((f32[3,16,16,16]{3,2,1,0:T(8,128)S(1)}, f32[3,16,16,16]{3,2,1,0:T(8,128)}, u32[]{:S(2)}) %copy-start.6) | copy-done | bytes 49176
  3.0 0.0 copy-start
  3.0 0.0 copy-start.1
  3.0 0.0 copy-start.2
  3.0 0.3 copy.12
  3.2 0.0 copy-start.4
  3.2 0.0 copy-done.3
  3.3 0.7 %copy-done = f32[3,2,32,512]{3,2,1,0:T(8,128)S(1)} copy-done((f32[3,2,32,512]{3,2,1,0:T(8,128)S(1)}, f32[3,2,32,512]{3,2,1,0:T(8,128)}, u32[]{:S(2)}) %copy-start) | copy-done | bytes 393240
  4.0 0.1 copy-done.1
  4.0 0.0 copy-done.2
  4.1 0.0 copy-done.4
  4.1 40.9 %shard_map.111 = (f32[3,2,32,512]{3,2,1,0:T(8,128)S(1)}, f32[2,32,512]{2,1,0:T(8,128)S(1)}, f32[2,2,32,512]{3,2,1,0:T(8,128)S(1)}, f32[3,16,16,16]{3,2,1,0:T(8,128)S(1)}) custom-call(f32[3,2,32,512]{3,2,1,0:T(8,128)S(1)} %copy-done, f32[2,32,512]{2,1,0:T(8,128)S(1)} %copy-done.2, f32[2,2,32,512]{3,2,1,0:T(8,128)S(1)} %copy-done.1, ...), custom_call_target="tpu_custom_call" | custom-call | tf_op jit(solution)/shard_map/pallas_call | solution.py:746
  45.0 1.0 %copy.15 = f32[3,16,16,16]{3,2,1,0:T(8,128)} copy(f32[3,16,16,16]{1,2,3,0:T(8,128)S(1)} %bitcast.7) | data formatting | bytes 98304
  46.0 0.7 %copy.19 = f32[3,2,32,512]{3,2,1,0:T(8,128)} copy(f32[3,2,32,512]{3,2,1,0:T(8,128)S(1)} %get-tuple-element.20) | data formatting | bytes 786432
  46.7 0.7 %copy.20 = f32[2,32,512]{2,1,0:T(8,128)} copy(f32[2,32,512]{2,1,0:T(8,128)S(1)} %get-tuple-element.21) | data formatting | bytes 262144
  47.4 0.7 %copy.21 = f32[2,2,32,512]{3,2,1,0:T(8,128)} copy(f32[2,2,32,512]{3,2,1,0:T(8,128)S(1)} %get-tuple-element.22) | data formatting | bytes 524288
Async XLA Ops:
  0.6 1.3 %copy-start.5 = (f32[3,16,16,16]{3,2,1,0:T(8,128)S(1)}, f32[3,16,16,16]{3,2,1,0:T(8,128)}, u32[]{:S(2)}) copy-start(f32[3,16,16,16]{3,2,1,0:T(8,128)} %param.14) | copy-start | bytes 147460
  2.0 1.0 %copy-start.6 = (f32[3,16,16,16]{3,2,1,0:T(8,128)S(1)}, f32[3,16,16,16]{3,2,1,0:T(8,128)}, u32[]{:S(2)}) copy-start(f32[3,16,16,16]{3,2,1,0:T(8,128)} %param.15) | copy-start | bytes 147460
  2.0 1.3 %copy-start.3 = (s32[1,16,256]{2,1,0:T(8,128)S(1)}, s32[1,16,256]{2,1,0:T(8,128)}, u32[]{:S(2)}) copy-start(s32[1,16,256]{2,1,0:T(8,128)} %zone_ref.1) | copy-start | bytes 49156
  3.0 1.0 %copy-start = (f32[3,2,32,512]{3,2,1,0:T(8,128)S(1)}, f32[3,2,32,512]{3,2,1,0:T(8,128)}, u32[]{:S(2)}) copy-start(f32[3,2,32,512]{3,2,1,0:T(8,128)} %melt_ref.1) | copy-start | bytes 1179652
  3.0 1.1 %copy-start.1 = (f32[2,2,32,512]{3,2,1,0:T(8,128)S(1)}, f32[2,2,32,512]{3,2,1,0:T(8,128)}, u32[]{:S(2)}) copy-start(f32[2,2,32,512]{3,2,1,0:T(8,128)} %eddy_ref.1) | copy-start | bytes 786436
  3.0 1.1 %copy-start.2 = (f32[2,32,512]{2,1,0:T(8,128)S(1)}, f32[2,32,512]{2,1,0:T(8,128)}, u32[]{:S(2)}) copy-start(f32[2,32,512]{2,1,0:T(8,128)} %heat_ref.1) | copy-start | bytes 393220
  3.2 0.8 %copy-start.4 = (f32[8]{0:T(128)S(1)}, f32[8]{0:T(128)}, u32[]{:S(2)}) copy-start(f32[8]{0:T(128)} %table_ref.1) | copy-start | bytes 100

commit v3 on v2

--- a/solution.py
+++ b/solution.py
@@ -399,14 +399,19 @@
         )
         return down, up
 
-    def start_pair(pair):
+    def start_down(pair):
         @pl.when(me > 0)
         def _():
             pair[0].start()
 
+    def start_up(pair):
         @pl.when(me < n - 1)
         def _():
             pair[1].start()
+
+    def start_pair(pair):
+        start_down(pair)
+        start_up(pair)
 
     def receive_pair(pair):
         @pl.when(me < n - 1)
@@ -428,7 +433,7 @@
 
     def spread(step, send, recv, send_sem, recv_sem):
         copies = []
-        for offset in range(1, n):
+        for offset in sorted(range(1, n), key=lambda o: abs(2 * o - n)):
             target = lax.rem(me + offset, n)
             copies.append(
                 pltpu.make_async_remote_copy(
@@ -561,15 +566,15 @@
         )
         loads[...] = times_left(double_rows, wide)
 
-    def advance_all(step, store):
+    def advance_plane(step, plane, store):
         block = fields[step]
         sub8 = iota((ROW, width), 0)
         lane8 = iota((ROW, width), 1)
 
-        def chunk(plane, index, carry):
-            low = pl.multiple_of(index * ROW, ROW)
-            at = pl.multiple_of(index * ROW + ROW, ROW)
-            high = pl.multiple_of(index * ROW + 2 * ROW, ROW)
+        def chunk(index):
+            low = index * ROW
+            at = low + ROW
+            high = at + ROW
             here = pl.ds(at, ROW)
             centre = [block[f, plane, here, :] for f in range(6)]
             kinetic, dissip = centre[4], centre[5]
@@ -597,7 +602,7 @@
                     square = grad_x * grad_x + grad_y * grad_y + grad_z * grad_z
                     strain = square if strain is None else strain + square
                 if f < 4:
-                    src = loads[pl.ds(pl.multiple_of(f * fine_rows + index * ROW, ROW), ROW), :]
+                    src = loads[pl.ds(f * fine_rows + index * ROW, ROW), :]
                 elif f == 4:
                     produce = eddy * strain
                     src = produce - dissip
@@ -616,16 +621,15 @@
                 store(
                     f, plane, index, mid + time_step * (spread_by * laplace - transport + src)
                 )
-            return carry
-
-        for plane in (1, 2):
-            lax.fori_loop(0, fine_rows // ROW, functools.partial(chunk, plane), 0)
+
+        for index in range(fine_rows // ROW):
+            chunk(index)
 
     def store_mid(f, plane, index, value):
-        fields1[f, plane, pl.ds(pl.multiple_of(index * ROW + ROW, ROW), ROW), :] = value
+        fields1[f, plane, pl.ds(index * ROW + ROW, ROW), :] = value
 
     def store_last(f, plane, index, value):
-        here = pl.ds(pl.multiple_of(index * ROW, ROW), ROW)
+        here = pl.ds(index * ROW, ROW)
         if f < 3:
             vel_out[f, plane - 1, here, :] = value
         elif f == 3:
@@ -654,27 +658,21 @@
         )
         return jnp.where(group < 3, whole, 0.0)
 
+    pl.semaphore_wait(barrier, n - 1)
+    halos = halo_copies(0)
+    start_pair(halos)
+    for fetch in fetches:
+        fetch.wait()
+    for row in (0, depth + 1):
+        pot_a[row] = blank(LANES)
+        pot_b[row] = blank(LANES)
+    planes = plane_copies(0)
     for step in range(STEPS):
-        if step == 0:
-            for fetch in fetches:
-                fetch.wait()
         restrict_and_window(step)
-        if step == 0:
-            pl.semaphore_wait(barrier, n - 1)
         forward = spread(step, send_f, recv_f, f_send_sem, f_recv_sem)
         for copy in forward:
             copy.start()
-        if step == 0:
-            halos = halo_copies(0)
-            start_pair(halos)
-        planes = plane_copies(step)
-        start_pair(planes)
         recv_f[step, me] = send_f[step, me]
-        if step == 0:
-            pot_a[0] = jnp.zeros((rows, LANES), jnp.float32)
-            pot_a[depth + 1] = jnp.zeros((rows, LANES), jnp.float32)
-            pot_b[0] = jnp.zeros((rows, LANES), jnp.float32)
-            pot_b[depth + 1] = jnp.zeros((rows, LANES), jnp.float32)
         receive_pair(halos)
         if step == 0:
             for z in range(depth):
@@ -688,14 +686,17 @@
             for z in range(depth):
                 sides = halo_in1[0, z // pack], halo_in1[1, z // pack]
                 pot_a[z + 1] = framed(pot_a[z + 1], *sides, z % pack)
-        sent_pair(halos)
         for copy in forward:
             copy.wait_recv()
+        if step == 0:
+            start_down(planes)
+        start_up(planes)
         relax_all(step)
         back = spread(step, send_b, recv_b, b_send_sem, b_recv_sem)
         for copy in back:
             copy.start()
         recv_b[step, me] = send_b[step, me]
+        sent_pair(halos)
         if step == 0:
             pack_potential()
             halos = halo_copies(1)
@@ -711,10 +712,18 @@
             copy.wait_recv()
         prolong_loads(step)
         receive_pair(planes)
-        advance_all(step, store_mid if step == 0 else store_last)
+        if step == 0:
+            following = plane_copies(1)
+            advance_plane(step, 1, store_mid)
+            start_down(following)
+            advance_plane(step, 2, store_mid)
+        else:
+            advance_plane(step, 1, store_last)
+            advance_plane(step, 2, store_last)
         for copy in back:
             copy.wait_send()
         sent_pair(planes)
+        planes = following
 
 
 def fused_on_device(

time: 48.2 us -> 51.6 us (1.071); the launches traced: 48.1 us -> 50.7 us
  Pallas kernels: 40.9 us -> 43.6 us
    pallas_call x1, Pallas kernels: 40.9 us -> 43.6 us  [fused_on_device(): pl.pallas_call(functools.partial(fused_kernel, n, xl), out_shape=(jax.Sha...]
where the time goes in v3:
time: 51.6 us; the launch traced here: 50.7 us
  Pallas kernels  43.6 us (84%)
  local copies, waits for them, and re-layouts  6.46 us (13%)
  between operations  0.71 us (1%)
    pallas_call x1, Pallas kernels, fused_on_device(): pl.pallas_call(functools.partial(fused_kernel, n, xl), out_shape=(jax.Sha...  43.6 us
    unnamed x21, local copies, waits for them, and re-layouts  6.46 us

profile of v3, /device:TPU:0, one launch (start us, length us, event | category | flops | bytes accessed | tf_op | source)
XLA Modules:
  0.0 50.7 jit_solution(7703560546383409739)
XLA Ops:
  0.6 0.0 copy-start.5
  0.6 1.3 %copy.13 = f32[3,16,16,16]{1,2,3,0:T(8,128)S(1)} copy(f32[3,16,16,16]{3,2,1,0:T(8,128)} %param.13) | data formatting | bytes 98304 | tf_op args[5]
  1.9 0.0 copy-done.5
  2.0 0.0 copy-start.6
  2.0 0.0 copy-start.3
  2.0 0.3 copy.14
  2.3 0.7 %copy-done.6 = f32[3,16,16,16]{3,2,1,0:T(8,128)S(1)} copy-done((f32[3,16,16,16]{3,2,1,0:T(8,128)S(1)}, f32[3,16,16,16]{3,2,1,0:T(8,128)}, u32[]{:S(2)}) %copy-start.6) | copy-done | bytes 49176
  3.0 0.0 copy-start
  3.0 0.0 copy-start.1
  3.0 0.0 copy-start.2
  3.0 0.3 copy.12
  3.2 0.0 copy-start.4
  3.2 0.0 copy-done.3
  3.3 0.7 %copy-done = f32[3,2,32,512]{3,2,1,0:T(8,128)S(1)} copy-done((f32[3,2,32,512]{3,2,1,0:T(8,128)S(1)}, f32[3,2,32,512]{3,2,1,0:T(8,128)}, u32[]{:S(2)}) %copy-start) | copy-done | bytes 393240
  4.0 0.1 copy-done.1
  4.0 0.0 copy-done.2
  4.1 0.0 copy-done.4
  4.1 43.6 %shard_map.111 = (f32[3,2,32,512]{3,2,1,0:T(8,128)S(1)}, f32[2,32,512]{2,1,0:T(8,128)S(1)}, f32[2,2,32,512]{3,2,1,0:T(8,128)S(1)}, f32[3,16,16,16]{3,2,1,0:T(8,128)S(1)}) custom-call(f32[3,2,32,512]{3,2,1,0:T(8,128)S(1)} %copy-done, f32[2,32,512]{2,1,0:T(8,128)S(1)} %copy-done.2, f32[2,2,32,512]{3,2,1,0:T(8,128)S(1)} %copy-done.1, ...), custom_call_target="tpu_custom_call" | custom-call | tf_op jit(solution)/shard_map/pallas_call | solution.py:755
  47.6 1.0 %copy.15 = f32[3,16,16,16]{3,2,1,0:T(8,128)} copy(f32[3,16,16,16]{1,2,3,0:T(8,128)S(1)} %bitcast.7) | data formatting | bytes 98304
  48.6 0.7 %copy.19 = f32[3,2,32,512]{3,2,1,0:T(8,128)} copy(f32[3,2,32,512]{3,2,1,0:T(8,128)S(1)} %get-tuple-element.20) | data formatting | bytes 786432
  49.4 0.7 %copy.20 = f32[2,32,512]{2,1,0:T(8,128)} copy(f32[2,32,512]{2,1,0:T(8,128)S(1)} %get-tuple-element.21) | data formatting | bytes 262144
  50.0 0.7 %copy.21 = f32[2,2,32,512]{3,2,1,0:T(8,128)} copy(f32[2,2,32,512]{3,2,1,0:T(8,128)S(1)} %get-tuple-element.22) | data formatting | bytes 524288
Async XLA Ops:
  0.6 1.3 %copy-start.5 = (f32[3,16,16,16]{3,2,1,0:T(8,128)S(1)}, f32[3,16,16,16]{3,2,1,0:T(8,128)}, u32[]{:S(2)}) copy-start(f32[3,16,16,16]{3,2,1,0:T(8,128)} %param.14) | copy-start | bytes 147460
  2.0 1.0 %copy-start.6 = (f32[3,16,16,16]{3,2,1,0:T(8,128)S(1)}, f32[3,16,16,16]{3,2,1,0:T(8,128)}, u32[]{:S(2)}) copy-start(f32[3,16,16,16]{3,2,1,0:T(8,128)} %param.15) | copy-start | bytes 147460
  2.0 1.3 %copy-start.3 = (s32[1,16,256]{2,1,0:T(8,128)S(1)}, s32[1,16,256]{2,1,0:T(8,128)}, u32[]{:S(2)}) copy-start(s32[1,16,256]{2,1,0:T(8,128)} %zone_ref.1) | copy-start | bytes 49156
  3.0 1.0 %copy-start = (f32[3,2,32,512]{3,2,1,0:T(8,128)S(1)}, f32[3,2,32,512]{3,2,1,0:T(8,128)}, u32[]{:S(2)}) copy-start(f32[3,2,32,512]{3,2,1,0:T(8,128)} %melt_ref.1) | copy-start | bytes 1179652
  3.0 1.1 %copy-start.1 = (f32[2,2,32,512]{3,2,1,0:T(8,128)S(1)}, f32[2,2,32,512]{3,2,1,0:T(8,128)}, u32[]{:S(2)}) copy-start(f32[2,2,32,512]{3,2,1,0:T(8,128)} %eddy_ref.1) | copy-start | bytes 786436
  3.0 1.1 %copy-start.2 = (f32[2,32,512]{2,1,0:T(8,128)S(1)}, f32[2,32,512]{2,1,0:T(8,128)}, u32[]{:S(2)}) copy-start(f32[2,32,512]{2,1,0:T(8,128)} %heat_ref.1) | copy-start | bytes 393220
  3.2 0.8 %copy-start.4 = (f32[8]{0:T(128)S(1)}, f32[8]{0:T(128)}, u32[]{:S(2)}) copy-start(f32[8]{0:T(128)} %table_ref.1) | copy-start | bytes 100

commit v4 on v3

--- a/solution.py
+++ b/solution.py
@@ -350,35 +350,50 @@
             )
 
     slot = inner // SWEEPS
-    for z in range(depth):
-        to_left = jnp.zeros((rows, LANES), jnp.float32)
-        to_right = to_left
-        for a in range(3):
-            value = own_ref[a, z]
-            to_left = jnp.where(slot == a, left_roll(value, SWEEPS - SWEEPS * a), to_left)
-            to_right = jnp.where(slot == a, left_roll(value, xl - SWEEPS * a), to_right)
-        halo_out0[0, z] = to_left
-        halo_out0[1, z] = to_right
-
-    def plane_copies(step):
-        block = fields[step]
-        down = pltpu.make_async_remote_copy(
-            src_ref=block.at[:, 1, body, :],
-            dst_ref=block.at[:, 3, body, :],
-            send_sem=p_send_sem.at[step, 0],
-            recv_sem=p_recv_sem.at[step, 0],
-            device_id=peer(me - 1),
+    pack = win // SWEEPS
+
+    def pack_halos(out, values):
+        for first in range(0, len(values), pack):
+            to_left = blank(LANES)
+            to_right = blank(LANES)
+            for k in range(pack):
+                value = values[first + k]()
+                to_left = jnp.where(slot == k, left_roll(value, SWEEPS - SWEEPS * k), to_left)
+                to_right = jnp.where(slot == k, left_roll(value, xl - SWEEPS * k), to_right)
+            out[0, first // pack] = to_left
+            out[1, first // pack] = to_right
+
+    pack_halos(
+        halo_out0,
+        [functools.partial(own_ref.__getitem__, (a, z)) for z in range(depth) for a in range(3)],
+    )
+
+    def face_copy(source, step, field, here, part, down):
+        side = 0 if down else 1
+        return pltpu.make_async_remote_copy(
+            src_ref=source,
+            dst_ref=fields[step].at[field, 3 if down else 0, here, :],
+            send_sem=p_send_sem.at[step, side, part],
+            recv_sem=p_recv_sem.at[step, side, part],
+            device_id=peer(me - 1 if down else me + 1),
             device_id_type=MESH,
         )
-        up = pltpu.make_async_remote_copy(
-            src_ref=block.at[:, 2, body, :],
-            dst_ref=block.at[:, 0, body, :],
-            send_sem=p_send_sem.at[step, 1],
-            recv_sem=p_recv_sem.at[step, 1],
-            device_id=peer(me + 1),
-            device_id_type=MESH,
-        )
-        return down, up
+
+    def first_faces(down):
+        at = 0 if down else 1
+        return [
+            face_copy(melt_ref.at[:, at], 0, slice(0, 3), body, 0, down),
+            face_copy(heat_ref.at[at], 0, 3, body, 1, down),
+            face_copy(eddy_ref.at[:, at], 0, slice(4, 6), body, 2, down),
+        ]
+
+    def later_faces(down):
+        copies = []
+        for part in range(fine_rows // ROW):
+            here = pl.ds(ROW + part * ROW, ROW)
+            mine = fields1.at[:, 1 if down else 2, here, :]
+            copies.append(face_copy(mine, 1, slice(0, 6), here, part, down))
+        return copies
 
     def halo_copies(step):
         down = pltpu.make_async_remote_copy(
@@ -397,39 +412,45 @@
             device_id=peer(me + 1),
             device_id_type=MESH,
         )
-        return down, up
-
-    def start_down(pair):
+        return [down], [up]
+
+    def start_down(copies):
         @pl.when(me > 0)
         def _():
-            pair[0].start()
-
-    def start_up(pair):
+            for copy in copies:
+                copy.start()
+
+    def start_up(copies):
         @pl.when(me < n - 1)
         def _():
-            pair[1].start()
+            for copy in copies:
+                copy.start()
 
     def start_pair(pair):
-        start_down(pair)
-        start_up(pair)
+        start_down(pair[0])
+        start_up(pair[1])
 
     def receive_pair(pair):
         @pl.when(me < n - 1)
         def _():
-            pair[0].wait_recv()
+            for copy in pair[0]:
+                copy.wait_recv()
 
         @pl.when(me > 0)
         def _():
-            pair[1].wait_recv()
+            for copy in pair[1]:
+                copy.wait_recv()
 
     def sent_pair(pair):
         @pl.when(me > 0)
         def _():
-            pair[0].wait_send()
+            for copy in pair[0]:
+                copy.wait_send()
 
         @pl.when(me < n - 1)
         def _():
-            pair[1].wait_send()
+            for copy in pair[1]:
+                copy.wait_send()
 
     def spread(step, send, recv, send_sem, recv_sem):
         copies = []
@@ -566,12 +587,12 @@
         )
         loads[...] = times_left(double_rows, wide)
 
-    def advance_plane(step, plane, store):
+    def advance_all(step, store, done):
         block = fields[step]
         sub8 = iota((ROW, width), 0)
         lane8 = iota((ROW, width), 1)
 
-        def chunk(index):
+        def chunk(plane, index):
             low = index * ROW
             at = low + ROW
             high = at + ROW
@@ -623,7 +644,9 @@
                 )
 
         for index in range(fine_rows // ROW):
-            chunk(index)
+            for plane in (1, 2):
+                chunk(plane, index)
+                done(plane, index)
 
     def store_mid(f, plane, index, value):
         fields1[f, plane, pl.ds(index * ROW + ROW, ROW), :] = value
@@ -637,36 +660,25 @@
         else:
             turb_out[f - 4, plane - 1, here, :] = value
 
-    pack = win // SWEEPS
-
-    def pack_potential():
-        for z in range(0, depth, pack):
-            to_left = jnp.zeros((rows, LANES), jnp.float32)
-            to_right = to_left
-            for k in range(pack):
-                value = pot_a[z + k + 1]
-                to_left = jnp.where(slot == k, left_roll(value, SWEEPS - SWEEPS * k), to_left)
-                to_right = jnp.where(slot == k, left_roll(value, xl - SWEEPS * k), to_right)
-            halo_out1[0, z // pack] = to_left
-            halo_out1[1, z // pack] = to_right
-
-    def framed(own, from_left, from_right, k):
-        left = left_roll(from_left, SWEEPS * k)
-        right = left_roll(from_right, SWEEPS * k - (win - SWEEPS))
+    def framed(own, arrived, index):
+        tile, k = divmod(index, pack)
+        left = left_roll(arrived[0, tile], SWEEPS * k)
+        right = left_roll(arrived[1, tile], SWEEPS * k - (win - SWEEPS))
         whole = jnp.where(
             inner < SWEEPS, left, jnp.where(inner >= win - SWEEPS, right, own)
         )
         return jnp.where(group < 3, whole, 0.0)
 
     pl.semaphore_wait(barrier, n - 1)
+    planes = first_faces(True), first_faces(False)
     halos = halo_copies(0)
     start_pair(halos)
+    start_pair(planes)
     for fetch in fetches:
         fetch.wait()
     for row in (0, depth + 1):
         pot_a[row] = blank(LANES)
         pot_b[row] = blank(LANES)
-    planes = plane_copies(0)
     for step in range(STEPS):
         restrict_and_window(step)
         forward = spread(step, send_f, recv_f, f_send_sem, f_recv_sem)
@@ -676,21 +688,16 @@
         receive_pair(halos)
         if step == 0:
             for z in range(depth):
-                sides = halo_in0[0, z], halo_in0[1, z]
-                pot_a[z + 1] = framed(own_ref[0, z], *sides, 0)
-                one, two, three = turned(framed(own_ref[1, z], *sides, 1))
+                pot_a[z + 1] = framed(own_ref[0, z], halo_in0, 3 * z)
+                one, two, three = turned(framed(own_ref[1, z], halo_in0, 3 * z + 1))
                 field1[z] = jnp.where(group < 2, one, two)
                 field2[z] = jnp.where(group == 0, two, three)
-                coil[z] = framed(own_ref[2, z], *sides, 2)
+                coil[z] = framed(own_ref[2, z], halo_in0, 3 * z + 2)
         else:
             for z in range(depth):
-                sides = halo_in1[0, z // pack], halo_in1[1, z // pack]
-                pot_a[z + 1] = framed(pot_a[z + 1], *sides, z % pack)
+                pot_a[z + 1] = framed(pot_a[z + 1], halo_in1, z)
         for copy in forward:
             copy.wait_recv()
-        if step == 0:
-            start_down(planes)
-        start_up(planes)
         relax_all(step)
         back = spread(step, send_b, recv_b, b_send_sem, b_recv_sem)
         for copy in back:
@@ -698,7 +705,10 @@
         recv_b[step, me] = send_b[step, me]
         sent_pair(halos)
         if step == 0:
-            pack_potential()
+            pack_halos(
+                halo_out1,
+                [functools.partial(pot_a.__getitem__, z + 1) for z in range(depth)],
+            )
             halos = halo_copies(1)
             start_pair(halos)
         else:
@@ -713,13 +723,17 @@
         prolong_loads(step)
         receive_pair(planes)
         if step == 0:
-            following = plane_copies(1)
-            advance_plane(step, 1, store_mid)
-            start_down(following)
-            advance_plane(step, 2, store_mid)
+            following = later_faces(True), later_faces(False)
+
+            def send_face(plane, index):
+                if plane == 1:
+                    start_down(following[0][index : index + 1])
+                else:
+                    start_up(following[1][index : index + 1])
+
+            advance_all(step, store_mid, send_face)
         else:
-            advance_plane(step, 1, store_last)
-            advance_plane(step, 2, store_last)
+            advance_all(step, store_last, lambda plane, index: None)
         for copy in back:
             copy.wait_send()
         sent_pair(planes)
@@ -779,8 +793,8 @@
             vmem(STEPS, n, rows // 2, LANES),
             vmem(STEPS, n, rows // 2, LANES),
             vmem(3, *plane),
-            vmem(2, *plane),
-            vmem(2, *plane),
+            vmem(2, 3 * depth * SWEEPS // win, rows, LANES),
+            vmem(2, 3 * depth * SWEEPS // win, rows, LANES),
             vmem(2, depth * SWEEPS // win, rows, LANES),
             vmem(2, depth * SWEEPS // win, rows, LANES),
             vmem(depth + 2, rows, LANES),
@@ -798,8 +812,8 @@
             dma((STEPS, n)),
             dma((STEPS, n)),
             dma((STEPS, n)),
-            dma((STEPS, 2)),
-            dma((STEPS, 2)),
+            dma((STEPS, 2, max(3, fine_rows // ROW))),
+            dma((STEPS, 2, max(3, fine_rows // ROW))),
             dma((STEPS, 2)),
             dma((STEPS, 2)),
         ],

time: 51.6 us -> 55.2 us (1.070); the launches traced: 50.7 us -> 55 us
  Pallas kernels: 43.6 us -> 47.9 us
    pallas_call x1, Pallas kernels: 43.6 us -> 47.9 us  [fused_on_device(): pl.pallas_call(functools.partial(fused_kernel, n, xl), out_shape=(jax.Sha...]
where the time goes in v4:
time: 55.2 us; the launch traced here: 55 us
  Pallas kernels  47.9 us (87%)
  local copies, waits for them, and re-layouts  6.46 us (12%)
  between operations  0.71 us (1%)
    pallas_call x1, Pallas kernels, fused_on_device(): pl.pallas_call(functools.partial(fused_kernel, n, xl), out_shape=(jax.Sha...  47.9 us
    unnamed x21, local copies, waits for them, and re-layouts  6.46 us

profile of v4, /device:TPU:0, one launch (start us, length us, event | category | flops | bytes accessed | tf_op | source)
XLA Modules:
  0.0 55.0 jit_solution(15782663171599285276)
XLA Ops:
  0.6 0.0 copy-start.5
  0.6 1.3 %copy.13 = f32[3,16,16,16]{1,2,3,0:T(8,128)S(1)} copy(f32[3,16,16,16]{3,2,1,0:T(8,128)} %param.13) | data formatting | bytes 98304 | tf_op args[5]
  1.9 0.0 copy-done.5
  2.0 0.0 copy-start.6
  2.0 0.0 copy-start.3
  2.0 0.3 copy.14
  2.3 0.7 %copy-done.6 = f32[3,16,16,16]{3,2,1,0:T(8,128)S(1)} copy-done((f32[3,16,16,16]{3,2,1,0:T(8,128)S(1)}, f32[3,16,16,16]{3,2,1,0:T(8,128)}, u32[]{:S(2)}) %copy-start.6) | copy-done | bytes 49176
  3.0 0.0 copy-start
  3.0 0.0 copy-start.1
  3.0 0.0 copy-start.2
  3.0 0.3 copy.12
  3.2 0.0 copy-start.4
  3.2 0.0 copy-done.3
  3.3 0.7 %copy-done = f32[3,2,32,512]{3,2,1,0:T(8,128)S(1)} copy-done((f32[3,2,32,512]{3,2,1,0:T(8,128)S(1)}, f32[3,2,32,512]{3,2,1,0:T(8,128)}, u32[]{:S(2)}) %copy-start) | copy-done | bytes 393240
  4.0 0.1 copy-done.1
  4.0 0.0 copy-done.2
  4.1 0.0 copy-done.4
  4.1 47.9 %shard_map.111 = (f32[3,2,32,512]{3,2,1,0:T(8,128)S(1)}, f32[2,32,512]{2,1,0:T(8,128)S(1)}, f32[2,2,32,512]{3,2,1,0:T(8,128)S(1)}, f32[3,16,16,16]{3,2,1,0:T(8,128)S(1)}) custom-call(f32[3,2,32,512]{3,2,1,0:T(8,128)S(1)} %copy-done, f32[2,32,512]{2,1,0:T(8,128)S(1)} %copy-done.2, f32[2,2,32,512]{3,2,1,0:T(8,128)S(1)} %copy-done.1, ...), custom_call_target="tpu_custom_call" | custom-call | tf_op jit(solution)/shard_map/pallas_call | solution.py:769
  51.9 1.0 %copy.15 = f32[3,16,16,16]{3,2,1,0:T(8,128)} copy(f32[3,16,16,16]{1,2,3,0:T(8,128)S(1)} %bitcast.7) | data formatting | bytes 98304
  52.9 0.7 %copy.19 = f32[3,2,32,512]{3,2,1,0:T(8,128)} copy(f32[3,2,32,512]{3,2,1,0:T(8,128)S(1)} %get-tuple-element.20) | data formatting | bytes 786432
  53.7 0.7 %copy.20 = f32[2,32,512]{2,1,0:T(8,128)} copy(f32[2,32,512]{2,1,0:T(8,128)S(1)} %get-tuple-element.21) | data formatting | bytes 262144
  54.3 0.7 %copy.21 = f32[2,2,32,512]{3,2,1,0:T(8,128)} copy(f32[2,2,32,512]{3,2,1,0:T(8,128)S(1)} %get-tuple-element.22) | data formatting | bytes 524288
Async XLA Ops:
  0.6 1.3 %copy-start.5 = (f32[3,16,16,16]{3,2,1,0:T(8,128)S(1)}, f32[3,16,16,16]{3,2,1,0:T(8,128)}, u32[]{:S(2)}) copy-start(f32[3,16,16,16]{3,2,1,0:T(8,128)} %param.14) | copy-start | bytes 147460
  2.0 1.0 %copy-start.6 = (f32[3,16,16,16]{3,2,1,0:T(8,128)S(1)}, f32[3,16,16,16]{3,2,1,0:T(8,128)}, u32[]{:S(2)}) copy-start(f32[3,16,16,16]{3,2,1,0:T(8,128)} %param.15) | copy-start | bytes 147460
  2.0 1.3 %copy-start.3 = (s32[1,16,256]{2,1,0:T(8,128)S(1)}, s32[1,16,256]{2,1,0:T(8,128)}, u32[]{:S(2)}) copy-start(s32[1,16,256]{2,1,0:T(8,128)} %zone_ref.1) | copy-start | bytes 49156
  3.0 1.0 %copy-start = (f32[3,2,32,512]{3,2,1,0:T(8,128)S(1)}, f32[3,2,32,512]{3,2,1,0:T(8,128)}, u32[]{:S(2)}) copy-start(f32[3,2,32,512]{3,2,1,0:T(8,128)} %melt_ref.1) | copy-start | bytes 1179652
  3.0 1.1 %copy-start.1 = (f32[2,2,32,512]{3,2,1,0:T(8,128)S(1)}, f32[2,2,32,512]{3,2,1,0:T(8,128)}, u32[]{:S(2)}) copy-start(f32[2,2,32,512]{3,2,1,0:T(8,128)} %eddy_ref.1) | copy-start | bytes 786436
  3.0 1.1 %copy-start.2 = (f32[2,32,512]{2,1,0:T(8,128)S(1)}, f32[2,32,512]{2,1,0:T(8,128)}, u32[]{:S(2)}) copy-start(f32[2,32,512]{2,1,0:T(8,128)} %heat_ref.1) | copy-start | bytes 393220
  3.2 0.8 %copy-start.4 = (f32[8]{0:T(128)S(1)}, f32[8]{0:T(128)}, u32[]{:S(2)}) copy-start(f32[8]{0:T(128)} %table_ref.1) | copy-start | bytes 100

commit v5 on v4

--- a/solution.py
+++ b/solution.py
@@ -368,31 +368,23 @@
         [functools.partial(own_ref.__getitem__, (a, z)) for z in range(depth) for a in range(3)],
     )
 
-    def face_copy(source, step, field, here, part, down):
+    pieces = fine_rows // ROW
+
+    def face_copies(step, down):
         side = 0 if down else 1
-        return pltpu.make_async_remote_copy(
-            src_ref=source,
-            dst_ref=fields[step].at[field, 3 if down else 0, here, :],
-            send_sem=p_send_sem.at[step, side, part],
-            recv_sem=p_recv_sem.at[step, side, part],
-            device_id=peer(me - 1 if down else me + 1),
-            device_id_type=MESH,
-        )
-
-    def first_faces(down):
-        at = 0 if down else 1
-        return [
-            face_copy(melt_ref.at[:, at], 0, slice(0, 3), body, 0, down),
-            face_copy(heat_ref.at[at], 0, 3, body, 1, down),
-            face_copy(eddy_ref.at[:, at], 0, slice(4, 6), body, 2, down),
-        ]
-
-    def later_faces(down):
         copies = []
-        for part in range(fine_rows // ROW):
+        for part in range(pieces):
             here = pl.ds(ROW + part * ROW, ROW)
-            mine = fields1.at[:, 1 if down else 2, here, :]
-            copies.append(face_copy(mine, 1, slice(0, 6), here, part, down))
+            copies.append(
+                pltpu.make_async_remote_copy(
+                    src_ref=fields[step].at[:, 1 + side, here, :],
+                    dst_ref=fields[step].at[:, 3 - 3 * side, here, :],
+                    send_sem=p_send_sem.at[step, side, part],
+                    recv_sem=p_recv_sem.at[step, side, part],
+                    device_id=peer(me - 1 if down else me + 1),
+                    device_id_type=MESH,
+                )
+            )
         return copies
 
     def halo_copies(step):
@@ -431,15 +423,19 @@
         start_up(pair[1])
 
     def receive_pair(pair):
-        @pl.when(me < n - 1)
-        def _():
-            for copy in pair[0]:
-                copy.wait_recv()
-
-        @pl.when(me > 0)
-        def _():
-            for copy in pair[1]:
-                copy.wait_recv()
+        if pair[0]:
+
+            @pl.when(me < n - 1)
+            def _():
+                for copy in pair[0]:
+                    copy.wait_recv()
+
+        if pair[1]:
+
+            @pl.when(me > 0)
+            def _():
+                for copy in pair[1]:
+                    copy.wait_recv()
 
     def sent_pair(pair):
         @pl.when(me > 0)
@@ -587,7 +583,7 @@
         )
         loads[...] = times_left(double_rows, wide)
 
-    def advance_all(step, store, done):
+    def advance_all(step, store, ready, done):
         block = fields[step]
         sub8 = iota((ROW, width), 0)
         lane8 = iota((ROW, width), 1)
@@ -645,6 +641,7 @@
 
         for index in range(fine_rows // ROW):
             for plane in (1, 2):
+                ready(plane, index)
                 chunk(plane, index)
                 done(plane, index)
 
@@ -670,10 +667,9 @@
         return jnp.where(group < 3, whole, 0.0)
 
     pl.semaphore_wait(barrier, n - 1)
-    planes = first_faces(True), first_faces(False)
+    planes = face_copies(0, True), face_copies(0, False)
     halos = halo_copies(0)
     start_pair(halos)
-    start_pair(planes)
     for fetch in fetches:
         fetch.wait()
     for row in (0, depth + 1):
@@ -684,6 +680,10 @@
         forward = spread(step, send_f, recv_f, f_send_sem, f_recv_sem)
         for copy in forward:
             copy.start()
+        if step == 0:
+            start_pair([side[: pieces // 2] for side in planes])
+        else:
+            start_pair([side[pieces // 2 :] for side in planes])
         recv_f[step, me] = send_f[step, me]
         receive_pair(halos)
         if step == 0:
@@ -705,6 +705,7 @@
         recv_b[step, me] = send_b[step, me]
         sent_pair(halos)
         if step == 0:
+            start_pair([side[pieces // 2 :] for side in planes])
             pack_halos(
                 halo_out1,
                 [functools.partial(pot_a.__getitem__, z + 1) for z in range(depth)],
@@ -721,19 +722,24 @@
         for copy in back:
             copy.wait_recv()
         prolong_loads(step)
-        receive_pair(planes)
         if step == 0:
-            following = later_faces(True), later_faces(False)
-
-            def send_face(plane, index):
-                if plane == 1:
-                    start_down(following[0][index : index + 1])
-                else:
-                    start_up(following[1][index : index + 1])
-
-            advance_all(step, store_mid, send_face)
-        else:
-            advance_all(step, store_last, lambda plane, index: None)
+            following = face_copies(1, True), face_copies(1, False)
+
+        def ready(plane, index):
+            if plane == 1:
+                receive_pair([[], planes[1][index : index + 1]])
+            else:
+                receive_pair([planes[0][index : index + 1], []])
+
+        def done(plane, index):
+            if step > 0 or index >= pieces // 2:
+                return
+            if plane == 1:
+                start_down(following[0][index : index + 1])
+            else:
+                start_up(following[1][index : index + 1])
+
+        advance_all(step, store_mid if step == 0 else store_last, ready, done)
         for copy in back:
             copy.wait_send()
         sent_pair(planes)
@@ -812,8 +818,8 @@
             dma((STEPS, n)),
             dma((STEPS, n)),
             dma((STEPS, n)),
-            dma((STEPS, 2, max(3, fine_rows // ROW))),
-            dma((STEPS, 2, max(3, fine_rows // ROW))),
+            dma((STEPS, 2, fine_rows // ROW)),
+            dma((STEPS, 2, fine_rows // ROW)),
             dma((STEPS, 2)),
             dma((STEPS, 2)),
         ],

time: 55.2 us -> 48.1 us (0.87)
  Pallas kernels: 47.9 us -> 40.7 us
    pallas_call x1, Pallas kernels: 47.9 us -> 40.7 us  [fused_on_device(): pl.pallas_call(functools.partial(fused_kernel, n, xl), out_shape=(jax.Sha...]
where the time goes in v5:
time: 48.1 us; the launch traced here: 47.9 us
  Pallas kernels  40.7 us (85%)
  local copies, waits for them, and re-layouts  6.46 us (13%)
  between operations  0.71 us (1%)
    pallas_call x1, Pallas kernels, fused_on_device(): pl.pallas_call(functools.partial(fused_kernel, n, xl), out_shape=(jax.Sha...  40.7 us
    unnamed x21, local copies, waits for them, and re-layouts  6.46 us

profile of v5, /device:TPU:0, one launch (start us, length us, event | category | flops | bytes accessed | tf_op | source)
XLA Modules:
  0.0 47.9 jit_solution(11718248721940306715)
XLA Ops:
  0.6 0.0 copy-start.5
  0.6 1.3 %copy.13 = f32[3,16,16,16]{1,2,3,0:T(8,128)S(1)} copy(f32[3,16,16,16]{3,2,1,0:T(8,128)} %param.13) | data formatting | bytes 98304 | tf_op args[5]
  1.9 0.0 copy-done.5
  2.0 0.0 copy-start.6
  2.0 0.0 copy-start.3
  2.0 0.3 copy.14
  2.3 0.7 %copy-done.6 = f32[3,16,16,16]{3,2,1,0:T(8,128)S(1)} copy-done((f32[3,16,16,16]{3,2,1,0:T(8,128)S(1)}, f32[3,16,16,16]{3,2,1,0:T(8,128)}, u32[]{:S(2)}) %copy-start.6) | copy-done | bytes 49176
  3.0 0.0 copy-start
  3.0 0.0 copy-start.1
  3.0 0.0 copy-start.2
  3.0 0.3 copy.12
  3.2 0.0 copy-start.4
  3.2 0.0 copy-done.3
  3.3 0.7 %copy-done = f32[3,2,32,512]{3,2,1,0:T(8,128)S(1)} copy-done((f32[3,2,32,512]{3,2,1,0:T(8,128)S(1)}, f32[3,2,32,512]{3,2,1,0:T(8,128)}, u32[]{:S(2)}) %copy-start) | copy-done | bytes 393240
  4.0 0.1 copy-done.1
  4.0 0.0 copy-done.2
  4.1 0.0 copy-done.4
  4.1 40.7 %shard_map.111 = (f32[3,2,32,512]{3,2,1,0:T(8,128)S(1)}, f32[2,32,512]{2,1,0:T(8,128)S(1)}, f32[2,2,32,512]{3,2,1,0:T(8,128)S(1)}, f32[3,16,16,16]{3,2,1,0:T(8,128)S(1)}) custom-call(f32[3,2,32,512]{3,2,1,0:T(8,128)S(1)} %copy-done, f32[2,32,512]{2,1,0:T(8,128)S(1)} %copy-done.2, f32[2,2,32,512]{3,2,1,0:T(8,128)S(1)} %copy-done.1, ...), custom_call_target="tpu_custom_call" | custom-call | tf_op jit(solution)/shard_map/pallas_call | solution.py:775
  44.8 1.0 %copy.15 = f32[3,16,16,16]{3,2,1,0:T(8,128)} copy(f32[3,16,16,16]{1,2,3,0:T(8,128)S(1)} %bitcast.7) | data formatting | bytes 98304
  45.8 0.7 %copy.19 = f32[3,2,32,512]{3,2,1,0:T(8,128)} copy(f32[3,2,32,512]{3,2,1,0:T(8,128)S(1)} %get-tuple-element.20) | data formatting | bytes 786432
  46.5 0.7 %copy.20 = f32[2,32,512]{2,1,0:T(8,128)} copy(f32[2,32,512]{2,1,0:T(8,128)S(1)} %get-tuple-element.21) | data formatting | bytes 262144
  47.2 0.7 %copy.21 = f32[2,2,32,512]{3,2,1,0:T(8,128)} copy(f32[2,2,32,512]{3,2,1,0:T(8,128)S(1)} %get-tuple-element.22) | data formatting | bytes 524288
Async XLA Ops:
  0.6 1.3 %copy-start.5 = (f32[3,16,16,16]{3,2,1,0:T(8,128)S(1)}, f32[3,16,16,16]{3,2,1,0:T(8,128)}, u32[]{:S(2)}) copy-start(f32[3,16,16,16]{3,2,1,0:T(8,128)} %param.14) | copy-start | bytes 147460
  2.0 1.0 %copy-start.6 = (f32[3,16,16,16]{3,2,1,0:T(8,128)S(1)}, f32[3,16,16,16]{3,2,1,0:T(8,128)}, u32[]{:S(2)}) copy-start(f32[3,16,16,16]{3,2,1,0:T(8,128)} %param.15) | copy-start | bytes 147460
  2.0 1.3 %copy-start.3 = (s32[1,16,256]{2,1,0:T(8,128)S(1)}, s32[1,16,256]{2,1,0:T(8,128)}, u32[]{:S(2)}) copy-start(s32[1,16,256]{2,1,0:T(8,128)} %zone_ref.1) | copy-start | bytes 49156
  3.0 1.0 %copy-start = (f32[3,2,32,512]{3,2,1,0:T(8,128)S(1)}, f32[3,2,32,512]{3,2,1,0:T(8,128)}, u32[]{:S(2)}) copy-start(f32[3,2,32,512]{3,2,1,0:T(8,128)} %melt_ref.1) | copy-start | bytes 1179652
  3.0 1.1 %copy-start.1 = (f32[2,2,32,512]{3,2,1,0:T(8,128)S(1)}, f32[2,2,32,512]{3,2,1,0:T(8,128)}, u32[]{:S(2)}) copy-start(f32[2,2,32,512]{3,2,1,0:T(8,128)} %eddy_ref.1) | copy-start | bytes 786436
  3.0 1.1 %copy-start.2 = (f32[2,32,512]{2,1,0:T(8,128)S(1)}, f32[2,32,512]{2,1,0:T(8,128)}, u32[]{:S(2)}) copy-start(f32[2,32,512]{2,1,0:T(8,128)} %heat_ref.1) | copy-start | bytes 393220
  3.2 0.8 %copy-start.4 = (f32[8]{0:T(128)S(1)}, f32[8]{0:T(128)}, u32[]{:S(2)}) copy-start(f32[8]{0:T(128)} %table_ref.1) | copy-start | bytes 100
